TPU v7x, 256 devices: a whole 4x4x8 slice. The times are simulated.
256 devices in a mesh: lat: 4 (over x_lo, core), lon: 64 (over x_hi, z, y).
Axes of the slice: x: 4 (x_hi: 2, x_lo: 2; x = x_hi * 2 + x_lo), y: 4, z: 8, core: 2. Of those that a mesh axis runs over, the one named last changes fastest.
Arguments:
- block_input: bfloat16 [4, 24, 1536, 192], P(None, 'lat', 'lon'), may hold values from -100 to 100
- cotangent: bfloat16 [4, 24, 1536, 192], P(None, 'lat', 'lon'), may hold values from -6 to 6
- first_gain: float32 [192], replicated, may hold values from 0.5 to 1.5
- second_gain: float32 [192], replicated, may hold values from 0.5 to 1.5
- input_weight: bfloat16 [192, 576], replicated, may hold values from -0.4375 to 0.4375
- output_weight: bfloat16 [192, 192], replicated, may hold values from -0.4375 to 0.4375
- up_weight: bfloat16 [192, 768], replicated, may hold values from -0.4375 to 0.4375
- down_weight: bfloat16 [768, 192], replicated, may hold values from -0.21875 to 0.21875
- bias_table: float32 [2, 4, 6, 23, 144], P(None, 'lat'), may hold values from -4.5 to 300
Outputs:
- grad_input: bfloat16 [4, 24, 1536, 192], P(None, 'lat', 'lon')
- bias_grad: float32 [2, 4, 6, 23, 144], P(None, 'lat')
All inputs are finite; a program needn't handle non-finite values.
Results may differ from a plain program's by a relative error of at most 0.018.
Values may be sent and summed in bfloat16 or wider, within the bound.
A program may use at most 128 MiB of HBM per device.

v0:
```python
import jax
import jax.numpy as jnp
from jax import lax
from jax.sharding import PartitionSpec as P

HEADS = 6
WZ = 2
WH = 6
WW = 12


EPSILON = 1e-05
EXCLUDED = -1000000000.0


def from_behind(value, axis, steps):
    count = lax.axis_size(axis)
    pairs = [(source, (source + steps) % count) for source in range(count)]
    return lax.ppermute(value, axis, pairs)


def norm_rows(values, gain):
    average = jnp.mean(values, axis=-1, keepdims=True)
    centred = values - average
    spread = jnp.mean(centred * centred, axis=-1, keepdims=True)
    return centred * lax.rsqrt(spread + EPSILON) * gain


def first_norm(values, gain):
    return norm_rows(values, gain).astype(jnp.bfloat16)


def block_tail(values, attention, gain, up_weight, down_weight):
    channel_count = values.shape[-1]
    residual = values + attention.astype(jnp.float32)
    normed = norm_rows(residual, gain).astype(jnp.bfloat16)
    hidden = jnp.dot(
        normed.reshape(-1, channel_count), up_weight, preferred_element_type=jnp.float32
    )
    active = jax.nn.gelu(hidden, approximate=False).astype(jnp.bfloat16)
    mixed = jnp.dot(active, down_weight, preferred_element_type=jnp.float32)
    return residual + mixed.reshape(residual.shape)


def expand_bias(bias_table):
    zone_count, band_count, head_count = (
        bias_table.shape[0],
        bias_table.shape[1],
        bias_table.shape[2],
    )
    offsets = jnp.arange(WW, dtype=jnp.int32)
    relative = offsets[:, None] - offsets[None, :] + WW - 1
    selector = (
        relative[:, :, None] == jnp.arange(2 * WW - 1, dtype=jnp.int32)[None, None, :]
    ).astype(jnp.float32)
    table_parts = bias_table.reshape(zone_count, band_count, head_count, 2 * WW - 1, WZ, WZ, WH, WH)
    expanded = jnp.einsum(
        "abnrpqst,ejr->abnpseqtj", table_parts, selector, precision=lax.Precision.HIGHEST
    )
    return expanded.reshape(zone_count, band_count, head_count, WZ * WH * WW, WZ * WH * WW)


def region_labels(zone_count, band_count, row_start, height, level_count):
    level_index = jnp.arange(zone_count * WZ, dtype=jnp.int32).reshape(zone_count, 1, WZ, 1, 1)
    row_index = row_start + jnp.arange(band_count * WH, dtype=jnp.int32).reshape(
        1, band_count, 1, WH, 1
    )
    level_mark = (level_index >= level_count - WZ // 2).astype(jnp.int32)
    row_mark = (row_index >= height - WH // 2).astype(jnp.int32)
    labels = jnp.broadcast_to(2 * level_mark + row_mark, (zone_count, band_count, WZ, WH, WW))
    return labels.reshape(zone_count, band_count, WZ * WH * WW)


def attend(block, bias_table, input_weight, output_weight, row_start, height):
    level_count, row_count, column_count, channel_count = block.shape
    zone_count = level_count // WZ
    band_count = row_count // WH
    sector_count = column_count // WW
    window_size = WZ * WH * WW
    head_size = channel_count // HEADS
    windows = block.reshape(zone_count, WZ, band_count, WH, sector_count, WW, channel_count)
    windows = windows.transpose(0, 2, 4, 1, 3, 5, 6).reshape(-1, channel_count)
    projected = jnp.dot(windows, input_weight, preferred_element_type=jnp.float32).astype(
        jnp.bfloat16
    )
    projected = projected.reshape(
        zone_count, band_count, sector_count, window_size, 3, HEADS, head_size
    )
    queries = projected[:, :, :, :, 0].astype(jnp.float32)
    key_part = projected[:, :, :, :, 1].astype(jnp.float32)
    value_part = projected[:, :, :, :, 2].astype(jnp.float32)
    scores = jnp.einsum("abwqnd,abwknd->abwnqk", queries, key_part) * head_size ** (-0.5)
    scores = scores + expand_bias(bias_table)[:, :, None]
    labels = region_labels(zone_count, band_count, row_start, height, level_count)
    allowed = labels[:, :, :, None] == labels[:, :, None, :]
    scores = jnp.where(allowed[:, :, None, None], scores, EXCLUDED)
    largest = jnp.max(scores, axis=-1, keepdims=True)
    weights = jnp.exp(scores - largest)
    probs = (weights / jnp.sum(weights, axis=-1, keepdims=True)).astype(jnp.bfloat16)
    mixed = jnp.einsum("abwnqk,abwknd->abwqnd", probs.astype(jnp.float32), value_part).astype(
        jnp.bfloat16
    )
    output = jnp.dot(
        mixed.reshape(-1, channel_count), output_weight, preferred_element_type=jnp.float32
    ).astype(jnp.bfloat16)
    output = output.reshape(zone_count, band_count, sector_count, WZ, WH, WW, channel_count)
    return output.transpose(0, 3, 1, 4, 2, 5, 6).reshape(
        level_count, row_count, column_count, channel_count
    )


def turn(block, step):
    row_count, column_count = (block.shape[1], block.shape[2])
    lift = WH // 2
    slide = WW // 2
    block = jnp.roll(block, step * (WZ // 2), 0)
    if step < 0:
        row_edge = block[:, :lift]
    else:
        row_edge = block[:, row_count - lift :]
    arrived_rows = from_behind(row_edge, "lat", step)
    if step < 0:
        moved = jnp.concatenate([block[:, lift:], arrived_rows], axis=1)
    else:
        moved = jnp.concatenate([arrived_rows, block[:, : row_count - lift]], axis=1)
    if step < 0:
        column_edge = moved[:, :, :slide]
    else:
        column_edge = moved[:, :, column_count - slide :]
    arrived_columns = from_behind(column_edge, "lon", step)
    if step < 0:
        return jnp.concatenate([moved[:, :, slide:], arrived_columns], axis=2)
    return jnp.concatenate([arrived_columns, moved[:, :, : column_count - slide]], axis=2)


def on_device(
    block_input,
    cotangent,
    first_gain,
    second_gain,
    input_weight,
    output_weight,
    up_weight,
    down_weight,
    bias_table,
):
    row_total = block_input.shape[1]
    row_start = lax.axis_index("lat") * row_total
    height = row_total * lax.axis_size("lat")

    def local_norm(values):
        return first_norm(values, first_gain)

    def local_attend(rows_in, table_in):
        return attend(rows_in, table_in, input_weight, output_weight, row_start, height)

    def local_tail(values, extra):
        return block_tail(values, extra, second_gain, up_weight, down_weight)

    inputs_wide = block_input.astype(jnp.float32)
    normed, norm_back = jax.vjp(local_norm, inputs_wide)
    attention_rolled, attend_back = jax.vjp(local_attend, turn(normed, -1), bias_table)
    _, tail_back = jax.vjp(local_tail, inputs_wide, turn(attention_rolled, 1))
    grad_direct, grad_attention = tail_back(cotangent.astype(jnp.float32))
    grad_window, bias_part = attend_back(turn(grad_attention, -1))
    (grad_front,) = norm_back(turn(grad_window, 1))
    grad_input = (grad_front + grad_direct).astype(jnp.bfloat16)
    bias_grad = lax.psum(bias_part, "lon")
    return (grad_input, bias_grad)


def solution(mesh):
    in_specs = (
        P(None, "lat", "lon", None),
        P(None, "lat", "lon", None),
        P(),
        P(),
        P(),
        P(),
        P(),
        P(),
        P(None, "lat", None, None, None),
    )
    out_specs = (P(None, "lat", "lon", None), P(None, "lat", None, None, None))
    return jax.shard_map(
        on_device, mesh=mesh, in_specs=in_specs, out_specs=out_specs, check_vma=False
    )
```

profile of v0, /device:TPU:32, one launch (start us, length us, event | category | flops | bytes accessed | tf_op | source)
XLA Modules:
  0.0 871.0 jit_solution(3637605662456149911)
XLA Ops:
  7.2 1.3 convert_reduce_fusion.1
  8.5 1.4 fusion.143
  10.6 1.4 fusion.145
  12.7 1.0 collective-permute-start
  14.5 8.9 %convolution_bitcast_fusion = f32[2,1,6,2,6,12,2,6,12]{8,7,4,6,3,2,0,5,1:T(8,128)} fusion(f32[2,6,23,2,2,6,6]{2,0,6,5,4,3,1:T(2,128)S(1)} %bitcast.135, s32[12,12]{1,0:T(8,128)S(1)} %subtract_add_fusion), kind=kOutput, calls=%fused_computation.2 | convolution fusion | flops 68680944 | bytes 1154880 | tf_op jit(solution)/shard_map/jvp(abnrpqst,ejr->abnpseqtj)/dot_general | solution.py:57
  23.6 20.7 %copy.121 = f32[2,1,6,2,6,12,2,6,12]{5,4,3,8,7,6,2,0,1:T(8,128)} copy(f32[2,1,6,2,6,12,2,6,12]{8,7,4,6,3,2,0,5,1:T(8,128)} %convolution_bitcast_fusion) | data formatting | bytes 1990656 | tf_op jit(solution)/shard_map/jvp()/add | solution.py:93
  44.2 9.3 %reshape.329 = f32[2,6,144,144]{2,3,1,0:T(8,128)S(1)} reshape(f32[2,1,6,2,6,12,2,6,12]{5,4,3,8,7,6,2,0,1:T(8,128)} %copy.121) | data formatting | bytes 1990656 | tf_op jit(solution)/shard_map/jvp()/add | solution.py:93
  53.6 2.8 collective-permute-start.1
  56.6 1.8 collective-permute-done.1
  59.1 1.3 convolution_convert_fusion.2
  60.4 1.2 copy.86
  61.6 4.9 reshape.303
  67.4 1.0 fusion.11
  68.5 1.0 fusion.207
  70.2 3.1 convert_reduce_fusion
  73.3 1.2 copy-done.5
  77.2 4.6 collective-permute-done.2
  81.8 1.9 collective-permute-start.3
  83.7 1.3 convolution_convert_fusion.1
  85.0 4.1 collective-permute-done.3
  91.3 6.7 fusion.103
  98.0 1.2 copy.99
  100.1 1.8 fusion.212
  103.6 2.0 collective-permute-done.4
  105.7 2.3 collective-permute-start.5
  108.1 2.8 collective-permute-done.5
  110.9 0.9 pad_maximum_fusion.5
  111.8 2.0 reshape.316
  113.8 1.8 copy.101
  115.6 1.8 reshape.317
  117.4 1.9 convolution_convert_fusion.5
  119.3 2.0 reshape.318
  121.4 3.8 fusion.5
  125.2 1.6 fusion.209
  127.0 1.0 fusion.94
  128.0 1.0 fusion.97
  131.3 2.3 copy.106
  133.6 5.0 reshape.320
  138.6 1.5 convolution_convert_fusion.7
  140.3 1.0 copy.108
  141.3 1.2 reshape.322
  143.7 2.2 copy.109
  145.9 10.1 %broadcast_in_dim.83 = f32[2,1,6,2,6,12,2,6,12]{8,7,6,5,4,3,2,0,1:T(8,128)} reshape(f32[2,6,144,144]{3,2,1,0:T(8,128)} %copy.109) | data formatting | bytes 1990656 | tf_op jit(solution)/shard_map/transpose(jvp())/reshape;transpose(jvp())/broadcast_in_dim | solution.py:60
  156.0 17.1 %fusion.82 = f32[2,1,6,23,2,2,6,6]{3,7,6,5,4,2,0,1:T(8,128)S(1)} fusion(s32[12,12]{1,0:T(8,128)S(1)} %subtract_add_fusion, f32[2,1,6,2,6,12,2,6,12]{8,7,6,5,4,3,2,0,1:T(8,128)} %broadcast_in_dim.83), kind=kOutput, calls=%fused_computation.96 | convolution fusion | flops 68680944 | bytes 1154880 | tf_op jit(solution)/shard_map/transpose(jvp(abnrpqst,ejr->abnpseqtj))/dot_general | solution.py:57
  173.1 1.7 copy.111
  175.0 683.5 %all-reduce.5.cloned.1.call-done = f32[2,1,6,23,144]{3,0,4,2,1:T(2,128)} async-done(((f32[2,1,6,23,144]{3,0,4,2,1:T(2,128)}), f32[2,1,6,23,144]{3,0,4,2,1:T(2,128)}) %all-reduce.5.cloned.1.call-update) | async-done | bytes 158992 | tf_op jit(solution)/shard_map/psum | solution.py:168
  858.5 2.2 copy.113
  862.2 0.9 add_convert_fusion
  (152 shorter events, 18.2 us)
Async XLA Ops:
  7.2 76.5 %copy-start = (bf16[768,192]{0,1:T(8,128)(2,1)S(1)}, bf16[768,192]{0,1:T(8,128)(2,1)}, u32[]{:S(2)}) copy-start(bf16[768,192]{0,1:T(8,128)(2,1)} %param.16) | copy-start | bytes 884740
  7.2 6.5 copy-start.36
  7.2 851.3 %all-reduce.5.cloned.1.call-start = ((), (), s32[]{:S(2)}) async-start(), calls=%async_computation | async-start | bytes 1769472 | tf_op jit(solution)/shard_map/psum | solution.py:168
  8.5 5.2 copy-start.13
  10.6 3.1 copy-start.23
  12.7 40.9 %collective-permute-start = (bf16[4,3,24,192]{3,0,2,1:T(4,128)(2,1)S(1)}, bf16[4,3,24,192]{3,0,2,1:T(4,128)(2,1)S(1)}, u32[]{:S(2)}, u32[]{:S(2)}) collective-permute-start(bf16[4,3,24,192]{3,0,2,1:T(4,128)(2,1)S(1)} %get-tuple-element.25), channel_id=1, source_target_pairs={{0,192},{64,0},{128,64},{192,128},{1,193},{65,1},{129,65},{193,129... | collective-permute-start | bytes 331784 | tf_op jit(solution)/shard_map/ppermute | solution.py:19
  23.6 45.9 %copy-start.11 = (pred[2,144,144]{1,2,0:T(8,128)(4,1)}, pred[2,144,144]{1,2,0:T(8,128)(4,1)S(1)}, u32[]{:S(2)}) copy-start(pred[2,144,144]{1,2,0:T(8,128)(4,1)S(1)} %broadcast_compare_fusion) | copy-start | bytes 124420
  53.6 4.8 collective-permute-start.1
  67.4 1.0 copy-start.16
  67.4 1.0 copy-start.18
  67.4 5.9 copy-start.20
  68.4 1.8 copy-start.2
  68.5 1.8 copy-start.30
  70.2 3.1 copy-start.32
  73.3 1.2 copy-start.5
  74.5 1.0 copy-start.34
  76.1 7.7 copy-start.8
  76.5 12.7 %copy-start.4 = (bf16[4,6,24,192]{3,2,1,0:T(8,128)(2,1)S(1)}, bf16[4,6,24,192]{3,2,1,0:T(8,128)(2,1)}, u32[]{:S(2)}) copy-start(bf16[4,6,24,192]{3,2,1,0:T(8,128)(2,1)} %param.9) | copy-start | bytes 663556
  77.1 4.6 collective-permute-start.2
  81.8 7.3 collective-permute-start.3
  83.7 6.4 copy-start.40
  85.0 6.2 copy-start.26
  89.6 9.6 %copy-start.15 = (f32[4,6,24]{0,2,1:T(8,128)}, f32[4,6,24]{0,2,1:T(8,128)S(1)}, u32[]{:S(2)}) copy-start(f32[4,6,24]{0,2,1:T(8,128)S(1)} %broadcast_multiply_fusion) | copy-start | bytes 6916
  90.1 7.9 copy-start.27
  99.2 2.6 copy-start.9
  101.8 1.1 copy-start.33
  102.9 14.6 %copy-start.35 = (bf16[192,192]{1,0:T(8,128)(2,1)S(1)}, bf16[192,192]{1,0:T(8,128)(2,1)}, u32[]{:S(2)}) copy-start(bf16[192,192]{1,0:T(8,128)(2,1)} %param.14) | copy-start | bytes 221188
  102.9 2.8 collective-permute-start.4
  105.7 5.2 collective-permute-start.5
  111.8 9.5 %copy-start.12 = (pred[2,144,144]{1,2,0:T(8,128)(4,1)S(1)}, pred[2,144,144]{1,2,0:T(8,128)(4,1)}, u32[]{:S(2)}) copy-start(pred[2,144,144]{1,2,0:T(8,128)(4,1)} %copy-done.11) | copy-start | bytes 124420
  111.8 9.5 %copy-start.21 = (bf16[2,1,2,144,1,6,32]{3,2,0,6,5,4,1:T(2,128)(2,1)S(1)}, bf16[2,1,2,144,1,6,32]{3,2,0,6,5,4,1:T(2,128)(2,1)}, u32[]{:S(2)}) copy-start(bf16[2,1,2,144,1,6,32]{3,2,0,6,5,4,1:T(2,128)(2,1)} %copy-done.20) | copy-start | bytes 663556
  111.8 9.5 %copy-start.31 = (f32[2,2,6,144]{3,2,1,0:T(8,128)S(1)}, f32[2,2,6,144]{3,2,1,0:T(8,128)}, u32[]{:S(2)}) copy-start(f32[2,2,6,144]{3,2,1,0:T(8,128)} %copy-done.30) | copy-start | bytes 41476
  111.8 9.5 %copy-start.38 = (f32[2,2,6,144]{3,2,1,0:T(8,128)S(1)}, f32[2,2,6,144]{3,2,1,0:T(8,128)}, u32[]{:S(2)}) copy-start(f32[2,2,6,144]{3,2,1,0:T(8,128)} %multiply_divide_fusion) | copy-start | bytes 41476
  121.3 3.9 copy-start.3
  125.2 1.7 copy-start.37
  125.2 1.7 copy-start.7
  125.2 1.7 copy-start.19
  127.9 1.5 copy-start.6
  127.9 1.5 copy-start.22
  131.3 7.3 copy-start.25
  143.6 31.2 %collective-permute-start.6 = (bf16[4,3,24,192]{3,0,2,1:T(4,128)(2,1)}, bf16[4,3,24,192]{3,0,2,1:T(4,128)(2,1)S(1)}, u32[]{:S(2)}, u32[]{:S(2)}) collective-permute-start(bf16[4,3,24,192]{3,0,2,1:T(4,128)(2,1)} %fusion.159), channel_id=1, source_target_pairs={{0,64},{64,128},{128,192},{192,0},{1,65},{65,129},{129,193},{193,1... | collective-permute-start | bytes 331784 | tf_op jit(solution)/shard_map/ppermute | solution.py:19
  174.8 685.9 %copy-start.14 = (f32[4,6,24]{0,2,1:T(8,128)S(1)}, f32[4,6,24]{0,2,1:T(8,128)}, u32[]{:S(2)}) copy-start(f32[4,6,24]{0,2,1:T(8,128)} %copy-done.13) | copy-start | bytes 6916
  174.8 685.9 %copy-start.39 = (f32[192]{0:T(256)S(1)}, f32[192]{0:T(256)}, u32[]{:S(2)}) copy-start(f32[192]{0:T(256)} %param.11) | copy-start | bytes 2308
  174.8 686.6 %copy-start.29 = (f32[4,6,24]{0,2,1:T(8,128)S(1)}, f32[4,6,24]{0,2,1:T(8,128)}, u32[]{:S(2)}) copy-start(f32[4,6,24]{0,2,1:T(8,128)} %copy-done.28) | copy-start | bytes 6916
  174.8 686.6 %copy-start.24 = (f32[4,6,24]{0,2,1:T(8,128)S(1)}, f32[4,6,24]{0,2,1:T(8,128)}, u32[]{:S(2)}) copy-start(f32[4,6,24]{0,2,1:T(8,128)} %copy-done.23) | copy-start | bytes 6916
  174.9 687.3 %copy-start.10 = (bf16[4,6,24,192]{3,2,1,0:T(8,128)(2,1)S(1)}, bf16[4,6,24,192]{3,2,1,0:T(8,128)(2,1)}, u32[]{:S(2)}) copy-start(bf16[4,6,24,192]{3,2,1,0:T(8,128)(2,1)} %param.10) | copy-start | bytes 663556
  174.9 685.8 %collective-permute-start.7 = (bf16[4,6,6,192]{3,0,2,1:T(4,128)(2,1)S(1)}, bf16[4,6,6,192]{3,0,2,1:T(4,128)(2,1)S(1)}, u32[]{:S(2)}, u32[]{:S(2)}) collective-permute-start(bf16[4,6,6,192]{3,0,2,1:T(4,128)(2,1)S(1)} %pad_maximum_fusion.8), channel_id=1, source_target_pairs={{0,1},{1,2},{2,3},{3,4},{4,5},{5,6},{6,7},{7,8},{8,9},{9,10},{10,1... | collective-permute-start | bytes 165896 | tf_op jit(solution)/shard_map/ppermute | solution.py:19
  861.4 2.5 copy-start.1
  (2 other events, 1.6 us)
Sparse Core Ops, SparseCore 0:
  174.9 683.5 all-reduce.4
where the time goes:
time: 884 us; the launch traced here: 871 us
  waiting for transfers between devices  699 us (79%)
  local copies, waits for them, and re-layouts  79.9 us (9%)
  matrix products  46.9 us (5%)
  other arithmetic  21.8 us (2%)
  between operations  15.1 us (2%)
    psum x1, waiting for transfers between devices, on_device(): bias_grad = lax.psum(bias_part, 'lon')  683 us
    add x2, local copies, waits for them, and re-layouts, attend(): scores = scores + expand_bias(bias_table)[:, :, None]  30 us
    dot_general x2, matrix products, expand_bias(): jnp.einsum('abnrpqst,ejr->abnpseqtj', table_parts, selector, precision=la...  26 us
  transfers between devices with their start and end apart: 9, of which 6 were waited for; matrix products, arithmetic and copies ran while one was open for 9% of the time, Pallas kernels for 0%

commit v1 on v0

v1 whole, which is shorter than its diff:
```python
import functools
import numpy as np
import jax
import jax.numpy as jnp
from jax import lax
from jax.experimental import pallas as pl
from jax.experimental.pallas import tpu as pltpu

BF = jnp.bfloat16
F32 = jnp.float32
HEADS, WZ, WH, WW = 6, 2, 6, 12
HD = 32
C = 192
FF = 768
N = 144
PS = WZ * WH
OFFS = 2 * WW - 1
LW = 384
EPS = 1e-05
SCALE = HD ** -0.5
NEG = -1e30


def nn(a, b):
    return lax.dot_general(a, b, (((1,), (0,)), ((), ())), preferred_element_type=F32)


def nt(a, b):
    return lax.dot_general(a, b, (((1,), (1,)), ((), ())), preferred_element_type=F32)


def tn(a, b):
    return lax.dot_general(a, b, (((0,), (0,)), ((), ())), preferred_element_type=F32)


def spread_consts():
    spread = np.zeros((N, PS, LW), np.float32)
    for p in range(WZ):
        for q in range(WZ):
            for s in range(WH):
                for t in range(WH):
                    m = ((p * WZ + q) * WH + s) * WH + t
                    for r in range(OFFS):
                        spread[m, q * WH + t, r * PS + p * WH + s] = 1
    pick = np.zeros((24, LW), np.float32)
    for r in range(OFFS):
        pick[r, r * PS:(r + 1) * PS] = 1
    return spread.reshape(N, PS * LW), pick


def normalize(v):
    centred = v - jnp.mean(v, axis=-1, keepdims=True)
    rs = lax.rsqrt(jnp.mean(centred * centred, axis=-1, keepdims=True) + EPS)
    return centred * rs, rs


def norm_back(g, xh, rs):
    return rs * (g - jnp.mean(g, axis=-1, keepdims=True) - xh * jnp.mean(g * xh, axis=-1, keepdims=True))


def gelu_slope(h):
    cdf = 0.5 + 0.5 * lax.erf(h * 0.7071067811865476)
    return cdf + h * (jnp.exp(-0.5 * (h * h)) * 0.3989422804014327)


def expand_bias(lat, tb_ref, spread_ref, pick_ref, t24, strips, bias):
    t24[...] = jnp.zeros_like(t24)
    t24[:, 0:OFFS, :] = tb_ref[...]
    table = t24[...].reshape(12 * 24, N)
    hi = table.astype(BF)
    rest = table - hi.astype(F32)
    mid = rest.astype(BF)
    low = (rest - mid.astype(F32)).astype(BF)
    pick = pick_ref[...][None]
    for qt in range(PS):
        sel = spread_ref[:, qt * LW:(qt + 1) * LW]
        wide = nn(hi, sel) + nn(mid, sel) + nn(low, sel)
        strips[:, qt, :] = jnp.sum(wide.reshape(12, 24, LW) * pick, axis=1)
    row = lax.broadcasted_iota(jnp.int32, (N, N), 0).astype(F32)
    col = lax.broadcasted_iota(jnp.int32, (N, N), 1).astype(F32)

    def place(v):
        ps = v - PS * jnp.floor((v + 0.5) * (1.0 / PS))
        upper = (ps >= WH).astype(F32)
        s = ps - WH * upper
        return upper, (s >= WH // 2).astype(F32)

    rp, rs = place(row)
    cp, cs = place(col)
    last_band = (lat == 3).astype(F32)
    apart_rows = jnp.abs(rs - cs) * last_band
    apart_levels = jnp.abs(rp - cp)

    def one(an, carry):
        strip = strips[an]
        top = jnp.where(an >= HEADS, 1.0, 0.0)
        apart = (apart_rows + apart_levels * top) > 0.5
        for j in range(WW):
            part = strip[0:PS, (WW - 1 - j) * PS:(WW - 1 - j) * PS + N]
            bias[an, j * PS:(j + 1) * PS, :] = part
        bias[an] = jnp.where(apart, NEG, bias[an])
        return carry

    lax.fori_loop(0, 12, one, 0)


def window_step(w, a, c, x, ct, g1, g2, wi_ref, wit, wk, wv, wo_ref, wu_ref, wd_ref,
                bias, qbd, dobd, probs, mixed, qkvt, dqkvt, dbias):
    x = x.astype(F32)
    ct32 = ct.astype(F32)
    xh1, rs1 = normalize(x)
    xn1 = (xh1 * g1).astype(BF)
    qkvt[...] = nt(wit[...], xn1).astype(BF)
    keys = nn(xn1, wk[...]).astype(BF)
    values = nn(xn1, wv[...]).astype(BF)
    for n in range(HEADS):
        qbd[n * HD:(n + 1) * HD, n * 256:n * 256 + N] = qkvt[n * HD:(n + 1) * HD, :]
    for n in range(HEADS):
        s = nn(keys, qbd[:, n * 256:n * 256 + N]) * SCALE + bias[a * HEADS + n]
        e = jnp.exp(s - jnp.max(s, axis=0, keepdims=True))
        p = (e * (1.0 / jnp.sum(e, axis=0, keepdims=True))).astype(BF)
        probs[n] = p
        vt = qkvt[2 * C + n * HD:2 * C + (n + 1) * HD, :]
        mixed[n * HD:(n + 1) * HD, :] = nn(vt, p).astype(BF)
    attn = tn(mixed[...], wo_ref[...]).astype(BF)
    y = x + attn.astype(F32)
    xh2, rs2 = normalize(y)
    xn2 = (xh2 * g2).astype(BF)
    dxn2 = jnp.zeros((N, C), F32)
    for f in range(FF // 256):
        up = wu_ref[:, f * 256:(f + 1) * 256]
        h = nn(xn2, up)
        da = nt(ct, wd_ref[f * 256:(f + 1) * 256, :])
        dh = (da * gelu_slope(h)).astype(BF)
        dxn2 = dxn2 + nt(dh, up)
    dy = ct32 + norm_back(dxn2 * g2, xh2, rs2)
    gattn = dy.astype(BF)
    dot_ = nt(wo_ref[...], gattn).astype(BF)
    for n in range(HEADS):
        dobd[n * HD:(n + 1) * HD, n * 256:n * 256 + N] = dot_[n * HD:(n + 1) * HD, :]
    for n in range(HEADS):
        r = slice(n * HD, (n + 1) * HD)
        dp = nn(values, dobd[:, n * 256:n * 256 + N])
        p = probs[n].astype(F32)
        pd = p * dp
        ds = pd - p * jnp.sum(pd, axis=0, keepdims=True)
        if c == 0:
            dbias[a * HEADS + n] = ds
        else:
            dbias[a * HEADS + n] += ds
        dsb = ds.astype(BF)
        dqkvt[n * HD:(n + 1) * HD, :] = (nn(qkvt[C + n * HD:C + (n + 1) * HD, :], dsb) * SCALE).astype(BF)
        dqkvt[C + n * HD:C + (n + 1) * HD, :] = (nt(qkvt[n * HD:(n + 1) * HD, :], dsb) * SCALE).astype(BF)
        dqkvt[2 * C + n * HD:2 * C + (n + 1) * HD, :] = nt(dot_[r, :], probs[n]).astype(BF)
    dxn1 = nn(wi_ref[...], dqkvt[...]).astype(BF).T.astype(F32)
    return (dy + norm_back(dxn1 * g1, xh1, rs1)).astype(BF)


def fold_bias(dbias, spread_ref, pick_ref, strips, folded):
    strips[...] = jnp.zeros_like(strips)

    def one(an, carry):
        total = jnp.zeros((PS, LW), F32)
        for j in range(WW):
            part = dbias[an, j * PS:(j + 1) * PS, :]
            lo = (WW - 1 - j) * PS
            total = total + jnp.pad(part, ((0, 0), (lo, LW - N - lo)))
        strips[an, 0:PS, :] = total
        return carry

    lax.fori_loop(0, 12, one, 0)
    pick = pick_ref[...][None]
    total = jnp.zeros((12 * 24, N), F32)
    for qt in range(PS):
        rows = strips[:, qt, :][:, None, :] * pick
        total = total + nt(rows.reshape(12 * 24, LW).astype(BF), spread_ref[:, qt * LW:(qt + 1) * LW])
    folded[...] = total.reshape(12, 24, N)


def prepare_weights(wi_ref, wit, wk, wv):
    wit[...] = wi_ref[...].T
    wk[...] = wi_ref[:, C:2 * C]
    wv[...] = wi_ref[:, 2 * C:3 * C]


def main_kernel(xw, cw, g1_ref, g2_ref, wi_ref, wo_ref, wu_ref, wd_ref, tb_ref, spread_ref, pick_ref,
                gi, red, t24, strips, bias, wit, wk, wv, qbd, dobd, probs, mixed, qkvt, dqkvt, dbias, folded):
    lat = lax.axis_index("lat")
    prepare_weights(wi_ref, wit, wk, wv)
    expand_bias(lat, tb_ref, spread_ref, pick_ref, t24, strips, bias)
    qbd[...] = jnp.zeros_like(qbd)
    dobd[...] = jnp.zeros_like(dobd)
    g1, g2 = g1_ref[...], g2_ref[...]

    def zone(a, carry):
        for c in range(2):
            w = a * 2 + c
            rows = pl.ds(pl.multiple_of(w * N, N), N)
            gi[rows, :] = window_step(
                w, a, c, xw[rows, :], cw[rows, :], g1, g2, wi_ref, wit, wk, wv, wo_ref, wu_ref, wd_ref, bias,
                qbd.at[c], dobd.at[c], probs.at[c], mixed.at[c], qkvt.at[c], dqkvt.at[c], dbias)
        return carry

    lax.fori_loop(0, 2, zone, 0)
    fold_bias(dbias, spread_ref, pick_ref, strips, folded)
    pack_fold(folded, red)


def pack_fold(folded, red):
    for s in range(6):
        red[s] = folded[2 * s:2 * s + 2, :, 0:128].reshape(48, 128).astype(BF)
    red[7] = jnp.zeros((48, 128), BF)
    lane = lax.broadcasted_iota(jnp.int32, (24, 128), 1)
    for half in range(2):
        total = jnp.zeros((24, 128), F32)
        for k in range(8 if half == 0 else 4):
            tail = jnp.concatenate([folded[half * 8 + k][:, 128:N], jnp.zeros((24, 112), F32)], axis=1)
            total = total + (pltpu.roll(tail, 16 * k, 1) if k else tail)
        red[6, half * 24:(half + 1) * 24, :] = total.astype(BF)


VM = pl.BlockSpec(memory_space=pltpu.VMEM)

MAIN_SCRATCH = [
    pltpu.VMEM((12, 24, N), F32),
    pltpu.VMEM((12, 16, LW), F32),
    pltpu.VMEM((12, N, N), F32),
    pltpu.VMEM((3 * C, C), BF),
    pltpu.VMEM((C, C), BF),
    pltpu.VMEM((C, C), BF),
    pltpu.VMEM((2, C, HEADS * 256), BF),
    pltpu.VMEM((2, C, HEADS * 256), BF),
    pltpu.VMEM((2, HEADS, N, N), BF),
    pltpu.VMEM((2, C, N), BF),
    pltpu.VMEM((2, 3 * C, N), BF),
    pltpu.VMEM((2, 3 * C, N), BF),
    pltpu.VMEM((12, N, N), F32),
    pltpu.VMEM((12, 24, N), F32),
]


def main_call(xw, cw, g1, g2, wi, wo, wu, wd, tb, spread, pick):
    return pl.pallas_call(
        main_kernel,
        out_shape=(jax.ShapeDtypeStruct((4 * N, C), BF), jax.ShapeDtypeStruct((8, 48, 128), BF)),
        in_specs=[VM] * 11,
        out_specs=(VM, VM),
        scratch_shapes=MAIN_SCRATCH,
        compiler_params=pltpu.CompilerParams(vmem_limit_bytes=48 * 1024 * 1024),
    )(xw, cw, g1, g2, wi, wo, wu, wd, tb, spread, pick)


PIECE0, PIECE1 = 80, 48
LAT0, LAT1, OWN1, LON1, DIAG1, ROWS = 80, 160, 208, 256, 304, 352
MESH = pl.DeviceIdType.MESH


def piece_consts():
    pack = np.zeros((2, ROWS, N), np.float32)
    place0 = np.zeros((N, LAT1), np.float32)
    place1 = np.zeros((N, ROWS - LAT1), np.float32)
    for p in range(2):
        for h in range(6):
            own = h >= 3
            s = h - 3 if own else h + 3
            for w in range(24):
                e = (w - 6) % 24
                if e < 12:
                    row = (0 if own else LAT0) + (e * 2 + p) * 3 + s % 3
                    place0[e * PS + p * WH + s, row] = 1
                else:
                    e -= 12
                    base = (OWN1 if own else LAT1) if e < 6 else (LON1 if own else DIAG1)
                    row = base + ((e % 6) * 2 + p) * 3 + s % 3
                    place1[e * PS + p * WH + s, row - LAT1] = 1
                pack[p, row, h * 24 + w] = 1
    return pack, place0, place1


def lat_lon():
    return lax.axis_index("lat"), lax.axis_index("lon")


def shifted(lat, lon, da, do):
    return lax.rem(lat + 4 + da, 4), lax.rem(lon + 64 + do, 64)


def in_kernel(x_ref, ct_ref, pack_ref, place0_ref, place1_ref, xw, cw, out_box, land, send_sem, recv_sem):
    lat, lon = lat_lon()
    barrier = pltpu.get_barrier_semaphore()
    for da, do in ((1, 0), (0, 1), (1, 1)):
        pl.semaphore_signal(barrier, inc=1, device_id=shifted(lat, lon, da, do), device_id_type=MESH)
    for a in range(2):
        for k, ref in enumerate((x_ref, ct_ref)):
            piece = (nn(pack_ref[0], ref[(2 * a + 1) % 4]) + nn(pack_ref[1], ref[(2 * a + 2) % 4])).astype(BF)
            lanes = slice(k * C, (k + 1) * C)
            land[a, 0:LAT0, lanes] = piece[0:LAT0]
            land[a, OWN1:LON1, lanes] = piece[OWN1:LON1]
            out_box[a, 0:128, lanes] = piece[LAT0:OWN1]
            out_box[a, 128:224, lanes] = piece[LON1:ROWS]
        if a == 0:
            pl.semaphore_wait(barrier, 3)
        for copy in in_copies(a, lat, lon, out_box, land, send_sem, recv_sem):
            copy.start()
    for a in range(2):
        for copy in in_copies(a, lat, lon, out_box, land, send_sem, recv_sem):
            copy.wait()
        first = nn(place0_ref[...], land[a, 0:LAT1, :]).astype(BF)
        second = nn(place1_ref[...], land[a, LAT1:ROWS, :]).astype(BF)
        for k, ref in enumerate((xw, cw)):
            ref[2 * a * N:(2 * a + 1) * N, :] = first[:, k * C:(k + 1) * C]
            ref[(2 * a + 1) * N:(2 * a + 2) * N, :] = second[:, k * C:(k + 1) * C]


def in_copies(a, lat, lon, out_box, land, send_sem, recv_sem):
    plan = ((0, 128, LAT0, (-1, 0)), (128, 48, LON1, (0, -1)), (176, 48, DIAG1, (-1, -1)))
    return [
        pltpu.make_async_remote_copy(
            src_ref=out_box.at[a, pl.ds(start, size)],
            dst_ref=land.at[a, pl.ds(target, size)],
            send_sem=send_sem.at[a, k],
            recv_sem=recv_sem.at[a, k],
            device_id=shifted(lat, lon, *step),
            device_id_type=MESH,
        )
        for k, (start, size, target, step) in enumerate(plan)
    ]


def back_copies(a, lat, lon, box, land, send_sem, recv_sem):
    plan = ((LAT0, 128, (1, 0)), (LON1, 48, (0, 1)), (DIAG1, 48, (1, 1)))
    return [
        pltpu.make_async_remote_copy(
            src_ref=box.at[a, pl.ds(start, size)],
            dst_ref=land.at[a, pl.ds(start, size)],
            send_sem=send_sem.at[a, k],
            recv_sem=recv_sem.at[a, k],
            device_id=shifted(lat, lon, *step),
            device_id_type=MESH,
        )
        for k, (start, size, step) in enumerate(plan)
    ]


def deep_peer(lon, d):
    high, z, y = lon // 32, lax.rem(lon // 4, 8), lax.rem(lon, 4)
    return (high * 8 + lax.rem(z + d, 8)) * 4 + y


def flat_peer(lon, d):
    z = lax.rem(lon // 4, 8)
    place = lax.rem((lon // 32) * 4 + lax.rem(lon, 4) + d, 8)
    return ((place // 4) * 8 + z) * 4 + lax.rem(place, 4)


def sum_copies(kind, lat, lon, src, dst, send_sem, recv_sem):
    z = lax.rem(lon // 4, 8)
    copies = []
    for d in range(1, 8):
        if kind == 0:
            peer = deep_peer(lon, d)
            source, target = src.at[lax.rem(z + d, 8)], dst.at[d - 1]
        elif kind == 1:
            peer = flat_peer(lon, d)
            source, target = src, dst.at[d - 1]
        else:
            peer = deep_peer(lon, d)
            source, target = src, dst.at[z]
        copies.append(pltpu.make_async_remote_copy(
            src_ref=source, dst_ref=target, send_sem=send_sem.at[kind, d - 1], recv_sem=recv_sem.at[kind, d - 1],
            device_id=(lat, peer), device_id_type=MESH))
    return copies


def add_up(own, slots):
    total = own.astype(F32)
    for d in range(7):
        total = total + slots[d].astype(F32)
    return total.astype(BF)


def out_kernel(gi_ref, red_ref, unpack_ref, unplace0_ref, unplace1_ref, gx_ref, gb_ref,
               box, land, slots1, part, slots2, whole, full, send_sem, recv_sem, sum_send, sum_recv):
    lat, lon = lat_lon()
    z = lax.rem(lon // 4, 8)
    barrier = pltpu.get_barrier_semaphore()
    for da, do in ((-1, 0), (0, -1), (-1, -1)):
        pl.semaphore_signal(barrier, inc=1, device_id=shifted(lat, lon, da, do), device_id_type=MESH)
    for d in range(1, 8):
        pl.semaphore_signal(barrier, inc=1, device_id=(lat, deep_peer(lon, d)), device_id_type=MESH)
        pl.semaphore_signal(barrier, inc=1, device_id=(lat, flat_peer(lon, d)), device_id_type=MESH)
    pl.semaphore_wait(barrier, 17)
    phase1 = sum_copies(0, lat, lon, red_ref, slots1, sum_send, sum_recv)
    for copy in phase1:
        copy.start()
    halos = [back_copies(a, lat, lon, box, land, send_sem, recv_sem) for a in range(2)]
    for a in range(2):
        first = nn(unplace0_ref[...], gi_ref[2 * a * N:(2 * a + 1) * N, :]).astype(BF)
        second = nn(unplace1_ref[...], gi_ref[(2 * a + 1) * N:(2 * a + 2) * N, :]).astype(BF)
        land[a, 0:LAT0, :] = first[0:LAT0]
        land[a, OWN1:LON1, :] = second[OWN1 - LAT1:LON1 - LAT1]
        box[a, LAT0:LAT1, :] = first[LAT0:LAT1]
        box[a, LAT1:OWN1, :] = second[0:OWN1 - LAT1]
        box[a, LON1:ROWS, :] = second[LON1 - LAT1:]
        for copy in halos[a]:
            copy.start()
    for copy in phase1:
        copy.wait()
    part[...] = add_up(red_ref[z], slots1)
    phase2 = sum_copies(1, lat, lon, part, slots2, sum_send, sum_recv)
    for copy in phase2:
        copy.start()
    for a in range(2):
        for copy in halos[a]:
            copy.wait()
        for p in range(2):
            gx_ref[(2 * a + 1 + p) % 4] = nn(unpack_ref[p], land[a]).astype(BF)
    for copy in phase2:
        copy.wait()
    whole[...] = add_up(part[...], slots2)
    phase3 = sum_copies(2, lat, lon, whole, full, sum_send, sum_recv)
    for copy in phase3:
        copy.start()
    full[z] = whole[...]
    for copy in phase3:
        copy.wait()
    for s in range(6):
        gb_ref[2 * s:2 * s + 2, :, 0:128] = full[s].astype(F32).reshape(2, 24, 128)[:, 0:OFFS]
    for half in range(2):
        tails = full[6, half * 24:(half + 1) * 24, :].astype(F32)
        for k in range(8 if half == 0 else 4):
            gb_ref[half * 8 + k, :, 128:N] = tails[0:OFFS, 16 * k:16 * (k + 1)]


def in_call(x, ct, pack, place0, place1):
    box = jax.ShapeDtypeStruct((4 * N, C), BF)
    return pl.pallas_call(
        in_kernel,
        out_shape=(box, box),
        in_specs=[VM] * 5,
        out_specs=(VM, VM),
        scratch_shapes=[
            pltpu.VMEM((2, 224, 2 * C), BF),
            pltpu.VMEM((2, ROWS, 2 * C), BF),
            pltpu.SemaphoreType.DMA((2, 3)),
            pltpu.SemaphoreType.DMA((2, 3)),
        ],
        compiler_params=pltpu.CompilerParams(collective_id=0, has_side_effects=True, vmem_limit_bytes=48 * 1024 * 1024),
    )(x, ct, pack, place0, place1)


def out_call(gi, red, unpack, unplace0, unplace1):
    return pl.pallas_call(
        out_kernel,
        out_shape=(jax.ShapeDtypeStruct((4, N, C), BF), jax.ShapeDtypeStruct((12, OFFS, N), F32)),
        in_specs=[VM] * 5,
        out_specs=(VM, VM),
        scratch_shapes=[
            pltpu.VMEM((2, ROWS, C), BF),
            pltpu.VMEM((2, ROWS, C), BF),
            pltpu.VMEM((7, 48, 128), BF),
            pltpu.VMEM((48, 128), BF),
            pltpu.VMEM((7, 48, 128), BF),
            pltpu.VMEM((48, 128), BF),
            pltpu.VMEM((8, 48, 128), BF),
            pltpu.SemaphoreType.DMA((2, 3)),
            pltpu.SemaphoreType.DMA((2, 3)),
            pltpu.SemaphoreType.DMA((3, 7)),
            pltpu.SemaphoreType.DMA((3, 7)),
        ],
        compiler_params=pltpu.CompilerParams(collective_id=1, has_side_effects=True, vmem_limit_bytes=48 * 1024 * 1024),
    )(gi, red, unpack, unplace0, unplace1)


def on_device(block_input, cotangent, first_gain, second_gain, input_weight, output_weight, up_weight,
              down_weight, bias_table):
    spread, pick = spread_consts()
    pack, place0, place1 = piece_consts()
    as_bf = lambda v: jnp.asarray(v, BF)
    xw, cw = in_call(block_input.reshape(4, N, C), cotangent.reshape(4, N, C), as_bf(pack), as_bf(place0), as_bf(place1))
    gi, red = main_call(xw, cw, first_gain[None], second_gain[None], input_weight, output_weight, up_weight,
                        down_weight, bias_table.reshape(12, OFFS, N), as_bf(spread), jnp.asarray(pick))
    gx, gb = out_call(gi, red, as_bf(pack.transpose(0, 2, 1)), as_bf(place0.T), as_bf(place1.T))
    return gx.reshape(block_input.shape), gb.reshape(bias_table.shape)


def solution(mesh):
    P = jax.sharding.PartitionSpec
    in_specs = (
        P(None, "lat", "lon", None),
        P(None, "lat", "lon", None),
        P(), P(), P(), P(), P(), P(),
        P(None, "lat", None, None, None),
    )
    out_specs = (P(None, "lat", "lon", None), P(None, "lat", None, None, None))
    return jax.shard_map(on_device, mesh=mesh, in_specs=in_specs, out_specs=out_specs, check_vma=False)
```

time: 884 us -> 77.1 us (0.09); the launches traced: 871 us -> 76.6 us
  waiting for transfers between devices: 699 us -> 0 us
  local copies, waits for them, and re-layouts: 79.9 us -> 12.6 us
  Pallas kernels: 0 us -> 63.3 us
  matrix products: 46.9 us -> 0 us
  other arithmetic: 21.8 us -> 0 us
  between operations: 15.1 us -> 0.73 us
    psum x1 -> x0, waiting for transfers between devices: 683 us -> none  [on_device(): bias_grad = lax.psum(bias_part, 'lon')]
    pallas_call x0 -> x3, Pallas kernels: none -> 63.3 us  [the longest x1 30.3 us: out_call(): pl.pallas_call(out_kernel, out_shape=(jax.ShapeDtypeStruct((4, N, C), BF)...]
    dot_general x14 -> x0, matrix products: 46.9 us -> none  [the longest x2 26 us: expand_bias(): jnp.einsum('abnrpqst,ejr->abnpseqtj', table_parts, selector, precision=la...]
    add x2 -> x0, local copies, waits for them, and re-layouts: 30 us -> none  [attend(): scores = scores + expand_bias(bias_table)[:, :, None]]
    reshape x12 -> x0, local copies, waits for them, and re-layouts: 18 us -> none  [the longest x2 9.96 us: attend(): projected.reshape(zone_count, band_count, sector_count, window_size, 3, H...]
    ppermute x8 -> x0, waiting for transfers between devices: 15.3 us -> none  [from_behind(): return lax.ppermute(value, axis, pairs)]
    reduce_sum x12 -> x0, other arithmetic: 14.1 us -> none  [the longest x1 3.09 us: attend(): largest = jnp.max(scores, axis=-1, keepdims=True)]
    broadcast_in_dim x3 -> x0, local copies, waits for them, and re-layouts: 10.3 us -> none  [the longest x1 10.1 us: expand_bias(): expanded.reshape(zone_count, band_count, head_count, WZ * WH * WW, WZ * W...]
  transfers between devices with their start and end apart: 9 -> 0, of which waited for: 6 -> 0; matrix products, arithmetic and copies ran while one was open for 9% -> 0% of each run, Pallas kernels for 0% -> 0%
where the time goes in v1:
time: 77.1 us; the launch traced here: 76.6 us
  Pallas kernels  63.3 us (82%)
  local copies, waits for them, and re-layouts  12.6 us (16%)
    pallas_call x1, Pallas kernels, out_call(): pl.pallas_call(out_kernel, out_shape=(jax.ShapeDtypeStruct((4, N, C), BF)...  30.3 us
    pallas_call x1, Pallas kernels, main_call(): pl.pallas_call(main_kernel, out_shape=(jax.ShapeDtypeStruct((4 * N, C), B...  26.3 us
    unnamed x34, local copies, waits for them, and re-layouts  12.6 us
    pallas_call x1, Pallas kernels, in_call(): pl.pallas_call(in_kernel, out_shape=(box, box), in_specs=[VM] * 5, out_sp...  6.67 us

profile of v1, /device:TPU:32, one launch (start us, length us, event | category | flops | bytes accessed | tf_op | source)
XLA Modules:
  0.0 76.6 jit_solution(2555790678721685449)
XLA Ops:
  0.6 0.0 copy-start.1
  0.6 0.0 copy-start
  0.7 1.1 %copy.21 = f32[2,1,6,23,144]{4,3,1,2,0:T(8,128)S(1)} copy(f32[2,1,6,23,144]{4,1,3,2,0:T(1,128)} %param.25) | data formatting | bytes 317952
  1.8 1.1 %copy.19.wd_ref = bf16[768,192]{1,0:T(8,128)(2,1)S(1)} copy(bf16[768,192]{0,1:T(8,128)(2,1)} %param.24) | data formatting | bytes 589824 | tf_op args[7]
  2.9 0.0 copy-done.1
  2.9 0.0 copy-start.2
  2.9 1.0 %copy-done.2 = bf16[4,6,24,192]{3,2,1,0:T(8,128)(2,1)S(1)} copy-done((bf16[4,6,24,192]{3,2,1,0:T(8,128)(2,1)S(1)}, bf16[4,6,24,192]{3,2,1,0:T(8,128)(2,1)}, u32[]{:S(2)}) %copy-start.2) | copy-done | bytes 221208
  3.9 0.0 copy-start.3
  3.9 1.0 %copy-done.3 = bf16[4,6,24,192]{3,2,1,0:T(8,128)(2,1)S(1)} copy-done((bf16[4,6,24,192]{3,2,1,0:T(8,128)(2,1)S(1)}, bf16[4,6,24,192]{3,2,1,0:T(8,128)(2,1)}, u32[]{:S(2)}) %copy-start.3) | copy-done | bytes 221208
  4.8 0.0 copy-start.10
  4.8 0.9 %copy-done.10 = bf16[144,192]{1,0:T(8,128)(2,1)S(1)} copy-done((bf16[144,192]{1,0:T(8,128)(2,1)S(1)}, bf16[144,192]{1,0:T(8,128)(2,1)}, u32[]{:S(2)}) %copy-start.10) | copy-done | bytes 55320
  5.7 0.0 copy-start.11
  5.7 0.9 %copy-done.11 = bf16[144,160]{1,0:T(8,128)(2,1)S(1)} copy-done((bf16[144,160]{1,0:T(8,128)(2,1)S(1)}, bf16[144,160]{1,0:T(8,128)(2,1)}, u32[]{:S(2)}) %copy-start.11) | copy-done | bytes 46104
  6.6 6.7 %shard_map.176 = (bf16[576,192]{1,0:T(8,128)(2,1)S(1)}, bf16[576,192]{1,0:T(8,128)(2,1)S(1)}) custom-call(bf16[4,144,192]{2,1,0:T(8,128)(2,1)S(1)} %bitcast.10, bf16[4,144,192]{2,1,0:T(8,128)(2,1)S(1)} %bitcast.11, bf16[2,352,144]{2,1,0:T(8,128)(2,1)S(1)} %copy-done.1, bf16[144,160]{1,0:T(8,128)(2,1)S(1)} %copy-done.11, bf16[144,192]{1,0:T(8,128)(2,1)S(1)} %copy-done.10), custom_call_target="tpu_custom_call" | custom-call | tf_op jit(solution)/shard_map/pallas_call | solution.py:437
  13.3 0.0 copy-done
  13.3 0.0 copy-start.4
  13.3 1.0 %copy-done.4 = bf16[192,768]{1,0:T(8,128)(2,1)S(1)} copy-done((bf16[192,768]{1,0:T(8,128)(2,1)S(1)}, bf16[192,768]{1,0:T(8,128)(2,1)}, u32[]{:S(2)}) %copy-start.4) | copy-done | bytes 294936
  14.3 0.0 copy-start.5
  14.3 0.9 %copy-done.5 = bf16[192,576]{1,0:T(8,128)(2,1)S(1)} copy-done((bf16[192,576]{1,0:T(8,128)(2,1)S(1)}, bf16[192,576]{1,0:T(8,128)(2,1)}, u32[]{:S(2)}) %copy-start.5) | copy-done | bytes 221208
  15.2 0.0 copy-start.7
  15.2 0.9 %copy-done.7 = bf16[192,192]{1,0:T(8,128)(2,1)S(1)} copy-done((bf16[192,192]{1,0:T(8,128)(2,1)S(1)}, bf16[192,192]{1,0:T(8,128)(2,1)}, u32[]{:S(2)}) %copy-start.7) | copy-done | bytes 73752
  16.1 0.0 copy-start.12
  16.1 0.8 copy-done.12
  16.9 0.0 copy-start.13
  16.9 0.7 copy-done.13
  17.5 0.0 copy-start.14
  17.5 0.7 copy-done.14
  18.2 0.0 copy-start.6
  18.2 0.0 copy-start.8
  18.2 0.0 copy-start.9
  18.2 26.3 %shard_map.177 = (bf16[576,192]{1,0:T(8,128)(2,1)S(1)}, bf16[8,48,128]{2,1,0:T(8,128)(2,1)S(1)}) custom-call(bf16[576,192]{1,0:T(8,128)(2,1)S(1)} %get-tuple-element.8.xw, bf16[576,192]{1,0:T(8,128)(2,1)S(1)} %get-tuple-element.9.cw, f32[1,192]{1,0:T(1,128)S(1)} %bitcast.12, f32[1,192]{1,0:T(1,128)S(1)} %bitcast.13, bf16[192,576]{1,0:T(8,128)(2,1)S(1)} %copy-done.5, ...), custom_call_target="tpu_custom_call" | custom-call | tf_op jit(solution)/shard_map/pallas_call | solution.py:243
  44.6 0.0 copy-done.6
  44.6 0.0 copy-done.8
  44.6 0.0 copy-done.9
  44.6 30.3 %shard_map.178 = (bf16[4,144,192]{2,1,0:T(8,128)(2,1)S(1)}, f32[12,23,144]{2,1,0:T(8,128)S(1)}) custom-call(bf16[576,192]{1,0:T(8,128)(2,1)S(1)} %get-tuple-element.10.gi_ref, bf16[8,48,128]{2,1,0:T(8,128)(2,1)S(1)} %get-tuple-element.11.red_ref, bf16[2,144,352]{2,1,0:T(8,128)(2,1)S(1)} %copy-done.6, bf16[160,144]{1,0:T(8,128)(2,1)S(1)} %copy-done.9, ...), custom_call_target="tpu_custom_call" | custom-call | tf_op jit(solution)/shard_map/pallas_call | solution.py:453
  74.9 1.0 %copy.20 = f32[2,1,6,23,144]{4,1,3,2,0:T(1,128)} copy(f32[2,1,6,23,144]{4,3,2,0,1:T(8,128)S(1)} %bitcast.9) | data formatting | bytes 317952
  75.9 0.7 copy.23
Async XLA Ops:
  0.6 2.3 %copy-start.1 = (bf16[2,352,144]{2,1,0:T(8,128)(2,1)S(1)}, bf16[2,352,144]{2,1,0:T(8,128)(2,1)}, u32[]{:S(2)}) copy-start(bf16[2,352,144]{2,1,0:T(8,128)(2,1)} %constant.16.clone.pack_ref) | copy-start | bytes 608260
  0.6 12.6 %copy-start = (bf16[144,4608]{1,0:T(8,128)(2,1)S(1)}, bf16[144,4608]{1,0:T(8,128)(2,1)}, u32[]{:S(2)}) copy-start(bf16[144,4608]{1,0:T(8,128)(2,1)} %constant.19.clone.spread_ref) | copy-start | bytes 3981316
  2.9 1.0 %copy-start.2 = (bf16[4,6,24,192]{3,2,1,0:T(8,128)(2,1)S(1)}, bf16[4,6,24,192]{3,2,1,0:T(8,128)(2,1)}, u32[]{:S(2)}) copy-start(bf16[4,6,24,192]{3,2,1,0:T(8,128)(2,1)} %param.17) | copy-start | bytes 663556
  3.9 1.0 %copy-start.3 = (bf16[4,6,24,192]{3,2,1,0:T(8,128)(2,1)S(1)}, bf16[4,6,24,192]{3,2,1,0:T(8,128)(2,1)}, u32[]{:S(2)}) copy-start(bf16[4,6,24,192]{3,2,1,0:T(8,128)(2,1)} %param.18) | copy-start | bytes 663556
  4.8 0.9 %copy-start.10 = (bf16[144,192]{1,0:T(8,128)(2,1)S(1)}, bf16[144,192]{1,0:T(8,128)(2,1)}, u32[]{:S(2)}) copy-start(bf16[144,192]{1,0:T(8,128)(2,1)} %constant.18.clone.place1_ref) | copy-start | bytes 165892
  5.7 0.9 %copy-start.11 = (bf16[144,160]{1,0:T(8,128)(2,1)S(1)}, bf16[144,160]{1,0:T(8,128)(2,1)}, u32[]{:S(2)}) copy-start(bf16[144,160]{1,0:T(8,128)(2,1)} %constant.17.clone.place0_ref) | copy-start | bytes 138244
  13.3 1.0 %copy-start.4 = (bf16[192,768]{1,0:T(8,128)(2,1)S(1)}, bf16[192,768]{1,0:T(8,128)(2,1)}, u32[]{:S(2)}) copy-start(bf16[192,768]{1,0:T(8,128)(2,1)} %wu_ref.1) | copy-start | bytes 884740
  14.3 0.9 %copy-start.5 = (bf16[192,576]{1,0:T(8,128)(2,1)S(1)}, bf16[192,576]{1,0:T(8,128)(2,1)}, u32[]{:S(2)}) copy-start(bf16[192,576]{1,0:T(8,128)(2,1)} %wi_ref.1) | copy-start | bytes 663556
  15.2 0.9 %copy-start.7 = (bf16[192,192]{1,0:T(8,128)(2,1)S(1)}, bf16[192,192]{1,0:T(8,128)(2,1)}, u32[]{:S(2)}) copy-start(bf16[192,192]{1,0:T(8,128)(2,1)} %wo_ref.1) | copy-start | bytes 221188
  16.1 0.8 %copy-start.12 = (f32[24,384]{1,0:T(8,128)S(1)}, f32[24,384]{1,0:T(8,128)}, u32[]{:S(2)}) copy-start(f32[24,384]{1,0:T(8,128)} %constant.20.clone.pick_ref) | copy-start | bytes 110596
  16.9 0.7 copy-start.13
  17.5 0.7 copy-start.14
  18.2 26.4 %copy-start.6 = (bf16[2,144,352]{2,1,0:T(8,128)(2,1)S(1)}, bf16[2,144,352]{2,1,0:T(8,128)(2,1)}, u32[]{:S(2)}) copy-start(bf16[2,144,352]{2,1,0:T(8,128)(2,1)} %constant.21.clone.unpack_ref) | copy-start | bytes 608260
  18.2 26.4 %copy-start.8 = (bf16[192,144]{1,0:T(8,128)(2,1)S(1)}, bf16[192,144]{1,0:T(8,128)(2,1)}, u32[]{:S(2)}) copy-start(bf16[192,144]{1,0:T(8,128)(2,1)} %constant.23.clone.unplace1_ref) | copy-start | bytes 165892
  18.2 26.4 %copy-start.9 = (bf16[160,144]{1,0:T(8,128)(2,1)S(1)}, bf16[160,144]{1,0:T(8,128)(2,1)}, u32[]{:S(2)}) copy-start(bf16[160,144]{1,0:T(8,128)(2,1)} %constant.22.clone.unplace0_ref) | copy-start | bytes 138244

commit v2 on v1

v2 whole, which is shorter than its diff:
```python
import functools
import numpy as np
import jax
import jax.numpy as jnp
from jax import lax
from jax.experimental import pallas as pl
from jax.experimental.pallas import tpu as pltpu

BF = jnp.bfloat16
F32 = jnp.float32
HEADS, WZ, WH, WW = 6, 2, 6, 12
HD = 32
C = 192
FF = 768
N = 144
PS = WZ * WH
OFFS = 2 * WW - 1
LW = 384
EPS = 1e-05
SCALE = HD ** -0.5
NEG = -1e30
LOG2E = 1.4426950408889634


def nn(a, b):
    return lax.dot_general(a, b, (((1,), (0,)), ((), ())), preferred_element_type=F32)


def nt(a, b):
    return lax.dot_general(a, b, (((1,), (1,)), ((), ())), preferred_element_type=F32)


def tn(a, b):
    return lax.dot_general(a, b, (((0,), (0,)), ((), ())), preferred_element_type=F32)


def spread_consts():
    spread = np.zeros((N, PS, LW), np.float32)
    for p in range(WZ):
        for q in range(WZ):
            for s in range(WH):
                for t in range(WH):
                    m = ((p * WZ + q) * WH + s) * WH + t
                    for r in range(OFFS):
                        spread[m, q * WH + t, r * PS + p * WH + s] = 1
    pick = np.zeros((24, LW), np.float32)
    for r in range(OFFS):
        pick[r, r * PS:(r + 1) * PS] = 1
    return spread.reshape(N, PS * LW), pick


def normalize(v):
    centred = v - jnp.mean(v, axis=-1, keepdims=True)
    rs = lax.rsqrt(jnp.mean(centred * centred, axis=-1, keepdims=True) + EPS)
    return centred * rs, rs


def norm_back(g, xh, rs):
    return rs * (g - jnp.mean(g, axis=-1, keepdims=True) - xh * jnp.mean(g * xh, axis=-1, keepdims=True))


def gelu_slope(h):
    cdf = 0.5 + 0.5 * lax.erf(h * 0.7071067811865476)
    return cdf + h * (jnp.exp(-0.5 * (h * h)) * 0.3989422804014327)


def expand_bias(lat, spread_ref, pick_ref, t24, strips, bias):
    table = t24[...].reshape(12 * 24, N)
    hi = table.astype(BF)
    rest = table - hi.astype(F32)
    mid = rest.astype(BF)
    low = (rest - mid.astype(F32)).astype(BF)
    pick = pick_ref[...][None] * LOG2E
    for qt in range(PS):
        sel = spread_ref[:, qt * LW:(qt + 1) * LW]
        wide = nn(hi, sel) + nn(mid, sel) + nn(low, sel)
        strips[:, qt, :] = jnp.sum(wide.reshape(12, 24, LW) * pick, axis=1)
    row = lax.broadcasted_iota(jnp.int32, (N, N), 0).astype(F32)
    col = lax.broadcasted_iota(jnp.int32, (N, N), 1).astype(F32)

    def place(v):
        ps = v - PS * jnp.floor((v + 0.5) * (1.0 / PS))
        upper = (ps >= WH).astype(F32)
        s = ps - WH * upper
        return upper, (s >= WH // 2).astype(F32)

    rp, rs = place(row)
    cp, cs = place(col)
    last_band = (lat == 3).astype(F32)
    apart_rows = jnp.abs(rs - cs) * last_band
    apart_levels = jnp.abs(rp - cp)
    for a in range(2):
        apart = apart_rows + apart_levels if a else apart_rows
        excluded = jnp.where(apart > 0.5, NEG, 0.0)
        for an in range(a * HEADS, (a + 1) * HEADS):
            strip = strips[an, 0:PS, :]
            for j in range(WW):
                lo = (WW - 1 - j) * PS
                rows = slice(j * PS, (j + 1) * PS)
                bias[an, rows, :] = strip[:, lo:lo + N] + excluded[rows]


GROUPS = ((0, 4), (4, 6))


def zone_step(a, x, ct, g1, g2, wq, wk, wv, wqkvt, wo_ref, wu_ref, wdt_ref,
              bias, masked, probs, dscores, mixed, dbias, hooks=()):
    halves = (slice(0, N), slice(N, 2 * N))
    heads = [slice(n * HD, (n + 1) * HD) for n in range(HEADS)]
    lane = lax.broadcasted_iota(jnp.int32, (1, 128), 1)
    picks = [((lane >= n * HD % 128) & (lane < n * HD % 128 + HD)).astype(F32) for n in range(HEADS)]
    picks16 = [v.astype(BF) for v in picks]

    def by_head(c, v, kind):
        for n in range(HEADS):
            if n < 4:
                masked[kind, c, n * N:(n + 1) * N, :] = v[:, 0:128] * picks16[n]
            else:
                masked[kind, c, n * N:(n + 1) * N, 0:64] = v[:, 128:C] * picks16[n][:, 0:64]

    x = x.astype(F32)
    xh1, rs1 = normalize(x)
    xn1 = (xh1 * g1).astype(BF)
    queries = nn(xn1, wq[...]).astype(BF)
    keys = nn(xn1, wk[...]).astype(BF)
    values = nn(xn1, wv[...]).astype(BF)
    qkvt = [nt(wqkvt[...], xn1[halves[c]]).astype(BF) for c in range(2)]
    for c in range(2):
        by_head(c, keys[halves[c]], 0)
        by_head(c, values[halves[c]], 1)
    for first, end in GROUPS:
        width = min(C, end * HD) - first * HD
        for c in range(2):
            s_all = nn(masked[0, c, first * N:end * N, 0:width], qkvt[c][first * HD:end * HD, :])
            for n in range(first, end):
                s = s_all[(n - first) * N:(n - first + 1) * N] * (SCALE * LOG2E) + bias[a * HEADS + n]
                e = jnp.exp2(s - jnp.max(s, axis=0, keepdims=True))
                p = (e * (1.0 / jnp.sum(e, axis=0, keepdims=True))).astype(BF)
                probs[c, n * N:(n + 1) * N, :] = p
                mixed[c, heads[n], :] = nn(qkvt[c][2 * C + n * HD:2 * C + (n + 1) * HD], p).astype(BF)
    if "attended" in hooks:
        hooks["attended"]()
    attn = jnp.concatenate([tn(mixed[c], wo_ref[...]) for c in range(2)], axis=0).astype(BF)
    y = x + attn.astype(F32)
    xh2, rs2 = normalize(y)
    xn2 = (xh2 * g2).astype(BF)
    dxn2 = jnp.zeros((2 * N, C), F32)
    for f in range(FF // 256):
        up = wu_ref[:, f * 256:(f + 1) * 256]
        h = nn(xn2, up)
        da = nn(ct, wdt_ref[:, f * 256:(f + 1) * 256])
        dh = (da * gelu_slope(h)).astype(BF)
        dxn2 = dxn2 + nt(dh, up)
    dy = ct.astype(F32) + norm_back(dxn2 * g2, xh2, rs2)
    gattn = dy.astype(BF)
    if "tail" in hooks:
        hooks["tail"]()
    dmix = nt(gattn, wo_ref[...]).astype(BF)
    dmixt = [nt(wo_ref[...], gattn[halves[c]]).astype(BF) for c in range(2)]
    dqs, dks, dvs = [[], []], [[], []], [[], []]
    for first, end in GROUPS:
        width = min(C, end * HD) - first * HD
        span = slice(first * HD, first * HD + width)
        parts = [[], []]
        for c in range(2):
            dp_all = nn(masked[1, c, first * N:end * N, 0:width], dmixt[c][span, :])
            for n in range(first, end):
                dp = dp_all[(n - first) * N:(n - first + 1) * N]
                p = probs[c, n * N:(n + 1) * N, :].astype(F32)
                pd = p * dp
                ds = pd - p * jnp.sum(pd, axis=0, keepdims=True)
                parts[c].append(ds)
                dsb = ds.astype(BF)
                dscores[c, n * N:(n + 1) * N, :] = dsb
                dqs[c].append(nn(qkvt[c][C + n * HD:C + (n + 1) * HD], dsb))
            dk_all = nn(dscores[c, first * N:end * N, :], queries[halves[c], span])
            dv_all = nn(probs[c, first * N:end * N, :], dmix[halves[c], span])
            for store, full in ((dks, dk_all), (dvs, dv_all)):
                total = jnp.zeros((N, width), F32)
                for n in range(first, end):
                    total = total + full[(n - first) * N:(n - first + 1) * N] * picks[n][:, 0:width]
                store[c].append(total)
        for n in range(first, end):
            dbias[a * HEADS + n] = parts[0][n - first] + parts[1][n - first]
    if "scores" in hooks:
        hooks["scores"]()
    dq = jnp.concatenate([(jnp.concatenate(dqs[c], axis=0) * SCALE).astype(BF).T for c in range(2)], axis=0)
    dk = (jnp.concatenate([jnp.concatenate(dks[c], axis=1) for c in range(2)], axis=0) * SCALE).astype(BF)
    dv = jnp.concatenate([jnp.concatenate(dvs[c], axis=1) for c in range(2)], axis=0).astype(BF)
    dxn1 = nt(dq, wq[...]) + nt(dk, wk[...]) + nt(dv, wv[...])
    return (dy + norm_back(dxn1.astype(BF).astype(F32) * g1, xh1, rs1)).astype(BF)


def fold_bias(a, dbias, spread_ref, pick_ref, strips, folded):
    for n in range(HEADS):
        total = jnp.zeros((PS, LW), F32)
        for j in range(WW):
            lo = (WW - 1 - j) * PS
            total = total + jnp.pad(dbias[a * HEADS + n, j * PS:(j + 1) * PS, :], ((0, 0), (lo, LW - N - lo)))
        strips[n, 0:PS, :] = total
    pick = pick_ref[...][None]
    total = jnp.zeros((HEADS * 24, N), F32)
    for qt in range(PS):
        rows = strips[0:HEADS, qt, :][:, None, :] * pick
        total = total + nt(rows.reshape(HEADS * 24, LW).astype(BF), spread_ref[:, qt * LW:(qt + 1) * LW])
    folded[...] = total.reshape(HEADS, 24, N)


def pack_fold(folded, red):
    flat = [folded[n, :, 0:128] for n in range(HEADS)]
    tails = jnp.zeros((24, 128), F32)
    for n in range(HEADS):
        tail = jnp.concatenate([folded[n, :, 128:N], jnp.zeros((24, 112), F32)], axis=1)
        tails = tails + (pltpu.roll(tail, 16 * n, 1) if n else tail)
    rows = jnp.concatenate(flat + [tails, jnp.zeros((256 - 7 * 24, 128), F32)], axis=0)
    red[...] = rows.astype(BF).reshape(8, 32, 128)


def unpack_fold(a, full, gb_ref):
    rows = full[...].astype(F32).reshape(256, 128)
    for n in range(HEADS):
        gb_ref[a * HEADS + n, :, 0:128] = rows[n * 24:n * 24 + OFFS]
        gb_ref[a * HEADS + n, :, 128:N] = rows[HEADS * 24:HEADS * 24 + OFFS, 16 * n:16 * (n + 1)]


def prepare_weights(wi_ref, wit, wq, wk, wv):
    wit[...] = wi_ref[...].T
    for k, ref in enumerate((wq, wk, wv)):
        ref[...] = wi_ref[:, k * C:(k + 1) * C]


VM = pl.BlockSpec(memory_space=pltpu.VMEM)

MAIN_SCRATCH = [
    pltpu.VMEM((12, 24, N), F32),
    pltpu.VMEM((12, 16, LW), F32),
    pltpu.VMEM((12, N, N), F32),
    pltpu.VMEM((3 * C, C), BF),
    pltpu.VMEM((C, C), BF),
    pltpu.VMEM((C, C), BF),
    pltpu.VMEM((C, C), BF),
    pltpu.VMEM((2, 2, HEADS * N, 128), BF),
    pltpu.VMEM((2, HEADS * N, N), BF),
    pltpu.VMEM((2, HEADS * N, N), BF),
    pltpu.VMEM((2, C, N), BF),
    pltpu.VMEM((12, N, N), F32),
    pltpu.VMEM((HEADS, 24, N), F32),
]


PIECE0, PIECE1 = 80, 48
LAT0, LAT1, OWN1, LON1, DIAG1, ROWS = 80, 160, 208, 256, 304, 352
MESH = pl.DeviceIdType.MESH


def piece_consts():
    pack = np.zeros((2, ROWS, N), np.float32)
    place0 = np.zeros((N, LAT1), np.float32)
    place1 = np.zeros((N, ROWS - LAT1), np.float32)
    for p in range(2):
        for h in range(6):
            own = h >= 3
            s = h - 3 if own else h + 3
            for w in range(24):
                e = (w - 6) % 24
                if e < 12:
                    row = (0 if own else LAT0) + (e * 2 + p) * 3 + s % 3
                    place0[e * PS + p * WH + s, row] = 1
                else:
                    e -= 12
                    base = (OWN1 if own else LAT1) if e < 6 else (LON1 if own else DIAG1)
                    row = base + ((e % 6) * 2 + p) * 3 + s % 3
                    place1[e * PS + p * WH + s, row - LAT1] = 1
                pack[p, row, h * 24 + w] = 1
    return pack, place0, place1


def lat_lon():
    return lax.axis_index("lat"), lax.axis_index("lon")


def shifted(lat, lon, da, do):
    return lax.rem(lat + 4 + da, 4), lax.rem(lon + 64 + do, 64)


def in_copies(a, lat, lon, out_box, land, send_sem, recv_sem):
    plan = ((0, 128, LAT0, (-1, 0)), (128, 48, LON1, (0, -1)), (176, 48, DIAG1, (-1, -1)))
    return [
        pltpu.make_async_remote_copy(
            src_ref=out_box.at[a, pl.ds(start, size)],
            dst_ref=land.at[a, pl.ds(target, size)],
            send_sem=send_sem.at[a, k],
            recv_sem=recv_sem.at[a, k],
            device_id=shifted(lat, lon, *step),
            device_id_type=MESH,
        )
        for k, (start, size, target, step) in enumerate(plan)
    ]


def back_copies(a, lat, lon, box, land, send_sem, recv_sem):
    plan = ((LAT0, 128, (1, 0)), (LON1, 48, (0, 1)), (DIAG1, 48, (1, 1)))
    return [
        pltpu.make_async_remote_copy(
            src_ref=box.at[a, pl.ds(start, size)],
            dst_ref=land.at[a, pl.ds(start, size)],
            send_sem=send_sem.at[a, k],
            recv_sem=recv_sem.at[a, k],
            device_id=shifted(lat, lon, *step),
            device_id_type=MESH,
        )
        for k, (start, size, step) in enumerate(plan)
    ]


def deep_peer(lon, d):
    high, z, y = lon // 32, lax.rem(lon // 4, 8), lax.rem(lon, 4)
    return (high * 8 + lax.rem(z + d, 8)) * 4 + y


def flat_peer(lon, d):
    z = lax.rem(lon // 4, 8)
    place = lax.rem((lon // 32) * 4 + lax.rem(lon, 4) + d, 8)
    return ((place // 4) * 8 + z) * 4 + lax.rem(place, 4)


def sum_copies(kind, a, lat, lon, src, dst, send_sem, recv_sem):
    z = lax.rem(lon // 4, 8)
    copies = []
    for d in range(1, 8):
        if kind == 0:
            peer = deep_peer(lon, d)
            source, target = src.at[a, lax.rem(z + d, 8)], dst.at[a, d - 1]
        elif kind == 1:
            peer = flat_peer(lon, d)
            source, target = src.at[a], dst.at[a, d - 1]
        else:
            peer = deep_peer(lon, d)
            source, target = src.at[a], dst.at[a, z]
        copies.append(pltpu.make_async_remote_copy(
            src_ref=source, dst_ref=target, send_sem=send_sem.at[a, kind, d - 1], recv_sem=recv_sem.at[a, kind, d - 1],
            device_id=(lat, peer), device_id_type=MESH))
    return copies


def add_up(own, slots):
    total = own.astype(F32)
    for d in range(7):
        total = total + slots[d].astype(F32)
    return total.astype(BF)


LOCAL = (
    ((4, N, C), BF), ((4, N, C), BF), ((2, ROWS, N), BF), ((N, LAT1), BF), ((N, ROWS - LAT1), BF),
    ((12, OFFS, N), F32), ((1, C), F32), ((1, C), F32), ((C, 3 * C), BF), ((C, C), BF), ((C, FF), BF), ((C, FF), BF),
    ((N, PS * LW), BF), ((24, LW), F32), ((2, N, ROWS), BF), ((LAT1, N), BF), ((ROWS - LAT1, N), BF),
)


def block_kernel(*refs):
    count = len(LOCAL)
    far = refs[:count]
    gx_ref, gb_ref = refs[count:count + 2]
    near = refs[count + 2:2 * count + 2]
    (x_ref, ct_ref, pack_ref, place0_ref, place1_ref, tb_ref, g1_ref, g2_ref, wi_ref, wo_ref, wu_ref, wdt_ref,
     spread_ref, pick_ref, unpack_ref, unplace0_ref, unplace1_ref) = near
    (t24, strips, bias, wit, wq, wk, wv, masked, probs, dscores, mixed, dbias, folded,
     out_box, land, back_box, back_land, red, slots1, part, slots2, whole, full,
     near_sem, in_send, in_recv, back_send, back_recv, sum_send, sum_recv) = refs[2 * count + 2:]
    lat, lon = lat_lon()
    z = lax.rem(lon // 4, 8)

    barrier = pltpu.get_barrier_semaphore()
    for da, do in ((1, 0), (0, 1), (1, 1), (-1, 0), (0, -1), (-1, -1)):
        pl.semaphore_signal(barrier, inc=1, device_id=shifted(lat, lon, da, do), device_id_type=MESH)
    for d in range(1, 8):
        pl.semaphore_signal(barrier, inc=1, device_id=(lat, deep_peer(lon, d)), device_id_type=MESH)
        pl.semaphore_signal(barrier, inc=1, device_id=(lat, flat_peer(lon, d)), device_id_type=MESH)
    fetches = [pltpu.make_async_copy(far[k], near[k], near_sem.at[k]) for k in range(count)]
    for fetch in fetches:
        fetch.start()
    for fetch in fetches[0:3]:
        fetch.wait()

    arrivals = []
    for a in range(2):
        for k, ref in enumerate((x_ref, ct_ref)):
            piece = (nn(pack_ref[0], ref[(2 * a + 1) % 4]) + nn(pack_ref[1], ref[(2 * a + 2) % 4])).astype(BF)
            lanes = slice(k * C, (k + 1) * C)
            land[a, 0:LAT0, lanes] = piece[0:LAT0]
            land[a, OWN1:LON1, lanes] = piece[OWN1:LON1]
            out_box[a, 0:128, lanes] = piece[LAT0:OWN1]
            out_box[a, 128:224, lanes] = piece[LON1:ROWS]
        if a == 0:
            pl.semaphore_wait(barrier, 20)
        arrivals.append(in_copies(a, lat, lon, out_box, land, in_send, in_recv))
        for copy in arrivals[a]:
            copy.start()

    for fetch in fetches[3:]:
        fetch.wait()
    t24[...] = jnp.zeros_like(t24)
    t24[:, 0:OFFS, :] = tb_ref[...]
    prepare_weights(wi_ref, wit, wq, wk, wv)
    expand_bias(lat, spread_ref, pick_ref, t24, strips, bias)
    g1, g2 = g1_ref[...], g2_ref[...]

    sums = [[sum_copies(kind, a, lat, lon, src, dst, sum_send, sum_recv)
             for kind, (src, dst) in enumerate(((red, slots1), (part, slots2), (whole, full)))] for a in range(2)]

    def sum_first(a):
        fold_bias(a, dbias, spread_ref, pick_ref, strips, folded)
        pack_fold(folded, red.at[a])
        for copy in sums[a][0]:
            copy.start()

    def sum_second(a):
        for copy in sums[a][0]:
            copy.wait()
        part[a] = add_up(red[a, z], slots1.at[a])
        for copy in sums[a][1]:
            copy.start()

    def sum_third(a):
        for copy in sums[a][1]:
            copy.wait()
        whole[a] = add_up(part[a], slots2.at[a])
        for copy in sums[a][2]:
            copy.start()
        full[a, z] = whole[a]

    def sum_last(a):
        for copy in sums[a][2]:
            copy.wait()
        unpack_fold(a, full.at[a], gb_ref)

    def zone(a, hooks):
        for copy in arrivals[a]:
            copy.wait()
        first = nn(place0_ref[...], land[a, 0:LAT1, :]).astype(BF)
        second = nn(place1_ref[...], land[a, LAT1:ROWS, :]).astype(BF)
        xw = jnp.concatenate([first[:, 0:C], second[:, 0:C]], axis=0)
        cw = jnp.concatenate([first[:, C:], second[:, C:]], axis=0)
        gi = zone_step(a, xw, cw, g1, g2, wq, wk, wv, wit, wo_ref, wu_ref, wdt_ref,
                       bias, masked, probs, dscores, mixed, dbias, hooks)
        first = nn(unplace0_ref[...], gi[0:N]).astype(BF)
        second = nn(unplace1_ref[...], gi[N:]).astype(BF)
        back_land[a, 0:LAT0, :] = first[0:LAT0]
        back_land[a, OWN1:LON1, :] = second[OWN1 - LAT1:LON1 - LAT1]
        back_box[a, LAT0:LAT1, :] = first[LAT0:LAT1]
        back_box[a, LAT1:OWN1, :] = second[0:OWN1 - LAT1]
        back_box[a, LON1:ROWS, :] = second[LON1 - LAT1:]
        copies = back_copies(a, lat, lon, back_box, back_land, back_send, back_recv)
        for copy in copies:
            copy.start()
        return copies

    def collect(a, copies):
        for copy in copies:
            copy.wait()
        for p in range(2):
            gx_ref[(2 * a + 1 + p) % 4] = nn(unpack_ref[p], back_land[a]).astype(BF)

    back0 = zone(0, {"scores": lambda: sum_first(0)})
    back1 = zone(1, {"attended": lambda: sum_second(0), "tail": lambda: sum_third(0), "scores": lambda: sum_first(1)})
    collect(0, back0)
    sum_last(0)
    sum_second(1)
    collect(1, back1)
    sum_third(1)
    sum_last(1)


def block_call(*operands):
    anywhere = pl.BlockSpec(memory_space=pl.ANY)
    dma = pltpu.SemaphoreType.DMA
    return pl.pallas_call(
        block_kernel,
        out_shape=(jax.ShapeDtypeStruct((4, N, C), BF), jax.ShapeDtypeStruct((12, OFFS, N), F32)),
        in_specs=[anywhere] * len(LOCAL),
        out_specs=(VM, VM),
        scratch_shapes=[pltpu.VMEM(*one) for one in LOCAL] + MAIN_SCRATCH + [
            pltpu.VMEM((2, 224, 2 * C), BF),
            pltpu.VMEM((2, ROWS, 2 * C), BF),
            pltpu.VMEM((2, ROWS, C), BF),
            pltpu.VMEM((2, ROWS, C), BF),
            pltpu.VMEM((2, 8, 32, 128), BF),
            pltpu.VMEM((2, 7, 32, 128), BF),
            pltpu.VMEM((2, 32, 128), BF),
            pltpu.VMEM((2, 7, 32, 128), BF),
            pltpu.VMEM((2, 32, 128), BF),
            pltpu.VMEM((2, 8, 32, 128), BF),
            dma((len(LOCAL),)), dma((2, 3)), dma((2, 3)), dma((2, 3)), dma((2, 3)), dma((2, 3, 7)), dma((2, 3, 7)),
        ],
        compiler_params=pltpu.CompilerParams(collective_id=0, has_side_effects=True, vmem_limit_bytes=60 * 1024 * 1024),
    )(*operands)


def on_device(block_input, cotangent, first_gain, second_gain, input_weight, output_weight, up_weight,
              down_weight, bias_table):
    spread, pick = spread_consts()
    pack, place0, place1 = piece_consts()
    as_bf = lambda v: jnp.asarray(v, BF)
    gx, gb = block_call(
        block_input.reshape(4, N, C), cotangent.reshape(4, N, C), as_bf(pack), as_bf(place0), as_bf(place1),
        bias_table.reshape(12, OFFS, N),
        first_gain[None], second_gain[None], input_weight, output_weight, up_weight, down_weight.T,
        as_bf(spread), jnp.asarray(pick), as_bf(pack.transpose(0, 2, 1)), as_bf(place0.T), as_bf(place1.T))
    return gx.reshape(block_input.shape), gb.reshape(bias_table.shape)


def solution(mesh):
    P = jax.sharding.PartitionSpec
    in_specs = (
        P(None, "lat", "lon", None),
        P(None, "lat", "lon", None),
        P(), P(), P(), P(), P(), P(),
        P(None, "lat", None, None, None),
    )
    out_specs = (P(None, "lat", "lon", None), P(None, "lat", None, None, None))
    return jax.shard_map(on_device, mesh=mesh, in_specs=in_specs, out_specs=out_specs, check_vma=False)
```

time: 77.1 us -> 56.5 us (0.73)
  Pallas kernels: 63.3 us -> 50.2 us
  local copies, waits for them, and re-layouts: 12.6 us -> 5.36 us
    pallas_call x3 -> x1, Pallas kernels: 63.3 us -> 50.2 us  [block_call(): pl.pallas_call(block_kernel, out_shape=(jax.ShapeDtypeStruct((4, N, C), B...]
    unnamed x34 -> x3, local copies, waits for them, and re-layouts: 12.6 us -> 5.36 us
where the time goes in v2:
time: 56.5 us; the launch traced here: 56.2 us
  Pallas kernels  50.2 us (89%)
  local copies, waits for them, and re-layouts  5.36 us (9%)
  between operations  0.64 us (1%)
    pallas_call x1, Pallas kernels, block_call(): pl.pallas_call(block_kernel, out_shape=(jax.ShapeDtypeStruct((4, N, C), B...  50.2 us
    unnamed x3, local copies, waits for them, and re-layouts  5.36 us

profile of v2, /device:TPU:32, one launch (start us, length us, event | category | flops | bytes accessed | tf_op | source)
XLA Modules:
  0.0 56.2 jit_solution(5407085779164210936)
XLA Ops:
  0.6 1.7 %copy.20 = f32[2,1,6,23,144]{4,3,1,2,0:T(8,128)} copy(f32[2,1,6,23,144]{4,1,3,2,0:T(1,128)} %param.25) | data formatting | bytes 317952
  2.3 50.2 %shard_map.176 = (bf16[4,144,192]{2,1,0:T(8,128)(2,1)}, f32[12,23,144]{2,1,0:T(8,128)}) custom-call(bf16[4,144,192]{2,1,0:T(8,128)(2,1)} %bitcast.9, bf16[4,144,192]{2,1,0:T(8,128)(2,1)} %bitcast.10, bf16[2,352,144]{2,1,0:T(8,128)(2,1)} %constant.16.clone.refs_2_, bf16[144,160]{1,0:T(8,128)(2,1)} %constant.17.clone.refs_3_, ...), custom_call_target="tpu_custom_call" | custom-call | tf_op jit(solution)/shard_map/pallas_call | solution.py:477
  52.5 2.0 %copy.19 = f32[2,1,6,23,144]{4,1,3,2,0:T(1,128)} copy(f32[2,1,6,23,144]{4,3,2,0,1:T(8,128)} %bitcast.13) | data formatting | bytes 317952
  54.5 1.7 %copy.22 = bf16[4,6,24,192]{3,2,1,0:T(8,128)(2,1)} copy(bf16[4,6,24,192]{3,2,1,0:T(8,128)(2,1)} %bitcast.12) | data formatting | bytes 442368

commit v3 on v2

--- a/solution.py
+++ b/solution.py
@@ -103,13 +103,19 @@
 GROUPS = ((0, 4), (4, 6))
 
 
-def zone_step(a, x, ct, g1, g2, wq, wk, wv, wqkvt, wo_ref, wu_ref, wdt_ref,
-              bias, masked, probs, dscores, mixed, dbias, hooks=()):
-    halves = (slice(0, N), slice(N, 2 * N))
-    heads = [slice(n * HD, (n + 1) * HD) for n in range(HEADS)]
+def halves():
+    return slice(0, N), slice(N, 2 * N)
+
+
+def head_picks():
     lane = lax.broadcasted_iota(jnp.int32, (1, 128), 1)
-    picks = [((lane >= n * HD % 128) & (lane < n * HD % 128 + HD)).astype(F32) for n in range(HEADS)]
-    picks16 = [v.astype(BF) for v in picks]
+    return [((lane >= n * HD % 128) & (lane < n * HD % 128 + HD)).astype(F32) for n in range(HEADS)]
+
+
+def zone_scores(a, x, ct, g1, g2, wq, wk, wv, wqkvt, wo_ref, wu_ref, wdt_ref,
+                bias, masked, probs, dscores, mixed, dbias):
+    half = halves()
+    picks16 = [v.astype(BF) for v in head_picks()]
 
     def by_head(c, v, kind):
         for n in range(HEADS):
@@ -121,13 +127,12 @@
     x = x.astype(F32)
     xh1, rs1 = normalize(x)
     xn1 = (xh1 * g1).astype(BF)
-    queries = nn(xn1, wq[...]).astype(BF)
     keys = nn(xn1, wk[...]).astype(BF)
     values = nn(xn1, wv[...]).astype(BF)
-    qkvt = [nt(wqkvt[...], xn1[halves[c]]).astype(BF) for c in range(2)]
+    qkvt = [nt(wqkvt[...], xn1[half[c]]).astype(BF) for c in range(2)]
     for c in range(2):
-        by_head(c, keys[halves[c]], 0)
-        by_head(c, values[halves[c]], 1)
+        by_head(c, keys[half[c]], 0)
+        by_head(c, values[half[c]], 1)
     for first, end in GROUPS:
         width = min(C, end * HD) - first * HD
         for c in range(2):
@@ -137,9 +142,7 @@
                 e = jnp.exp2(s - jnp.max(s, axis=0, keepdims=True))
                 p = (e * (1.0 / jnp.sum(e, axis=0, keepdims=True))).astype(BF)
                 probs[c, n * N:(n + 1) * N, :] = p
-                mixed[c, heads[n], :] = nn(qkvt[c][2 * C + n * HD:2 * C + (n + 1) * HD], p).astype(BF)
-    if "attended" in hooks:
-        hooks["attended"]()
+                mixed[c, n * HD:(n + 1) * HD, :] = nn(qkvt[c][2 * C + n * HD:2 * C + (n + 1) * HD], p).astype(BF)
     attn = jnp.concatenate([tn(mixed[c], wo_ref[...]) for c in range(2)], axis=0).astype(BF)
     y = x + attn.astype(F32)
     xh2, rs2 = normalize(y)
@@ -153,11 +156,7 @@
         dxn2 = dxn2 + nt(dh, up)
     dy = ct.astype(F32) + norm_back(dxn2 * g2, xh2, rs2)
     gattn = dy.astype(BF)
-    if "tail" in hooks:
-        hooks["tail"]()
-    dmix = nt(gattn, wo_ref[...]).astype(BF)
-    dmixt = [nt(wo_ref[...], gattn[halves[c]]).astype(BF) for c in range(2)]
-    dqs, dks, dvs = [[], []], [[], []], [[], []]
+    dmixt = [nt(wo_ref[...], gattn[half[c]]).astype(BF) for c in range(2)]
     for first, end in GROUPS:
         width = min(C, end * HD) - first * HD
         span = slice(first * HD, first * HD + width)
@@ -170,20 +169,32 @@
                 pd = p * dp
                 ds = pd - p * jnp.sum(pd, axis=0, keepdims=True)
                 parts[c].append(ds)
-                dsb = ds.astype(BF)
-                dscores[c, n * N:(n + 1) * N, :] = dsb
-                dqs[c].append(nn(qkvt[c][C + n * HD:C + (n + 1) * HD], dsb))
-            dk_all = nn(dscores[c, first * N:end * N, :], queries[halves[c], span])
-            dv_all = nn(probs[c, first * N:end * N, :], dmix[halves[c], span])
+                dscores[c, n * N:(n + 1) * N, :] = ds.astype(BF)
+        for n in range(first, end):
+            dbias[a * HEADS + n] = parts[0][n - first] + parts[1][n - first]
+    return xh1, rs1, xn1, [v[C:2 * C] for v in qkvt], dy, gattn
+
+
+def zone_finish(state, g1, wq, wk, wv, wo_ref, probs, dscores):
+    half = halves()
+    picks = head_picks()
+    xh1, rs1, xn1, keyst, dy, gattn = state
+    queries = nn(xn1, wq[...]).astype(BF)
+    dmix = nt(gattn, wo_ref[...]).astype(BF)
+    dqs, dks, dvs = [[], []], [[], []], [[], []]
+    for first, end in GROUPS:
+        width = min(C, end * HD) - first * HD
+        span = slice(first * HD, first * HD + width)
+        for c in range(2):
+            for n in range(first, end):
+                dqs[c].append(nn(keyst[c][n * HD:(n + 1) * HD], dscores[c, n * N:(n + 1) * N, :]))
+            dk_all = nn(dscores[c, first * N:end * N, :], queries[half[c], span])
+            dv_all = nn(probs[c, first * N:end * N, :], dmix[half[c], span])
             for store, full in ((dks, dk_all), (dvs, dv_all)):
                 total = jnp.zeros((N, width), F32)
                 for n in range(first, end):
                     total = total + full[(n - first) * N:(n - first + 1) * N] * picks[n][:, 0:width]
                 store[c].append(total)
-        for n in range(first, end):
-            dbias[a * HEADS + n] = parts[0][n - first] + parts[1][n - first]
-    if "scores" in hooks:
-        hooks["scores"]()
     dq = jnp.concatenate([(jnp.concatenate(dqs[c], axis=0) * SCALE).astype(BF).T for c in range(2)], axis=0)
     dk = (jnp.concatenate([jnp.concatenate(dks[c], axis=1) for c in range(2)], axis=0) * SCALE).astype(BF)
     dv = jnp.concatenate([jnp.concatenate(dvs[c], axis=1) for c in range(2)], axis=0).astype(BF)
@@ -239,10 +250,10 @@
     pltpu.VMEM((C, C), BF),
     pltpu.VMEM((C, C), BF),
     pltpu.VMEM((C, C), BF),
-    pltpu.VMEM((2, 2, HEADS * N, 128), BF),
-    pltpu.VMEM((2, HEADS * N, N), BF),
-    pltpu.VMEM((2, HEADS * N, N), BF),
-    pltpu.VMEM((2, C, N), BF),
+    pltpu.VMEM((2, 2, 2, HEADS * N, 128), BF),
+    pltpu.VMEM((2, 2, HEADS * N, N), BF),
+    pltpu.VMEM((2, 2, HEADS * N, N), BF),
+    pltpu.VMEM((2, 2, C, N), BF),
     pltpu.VMEM((12, N, N), F32),
     pltpu.VMEM((HEADS, 24, N), F32),
 ]
@@ -434,15 +445,18 @@
             copy.wait()
         unpack_fold(a, full.at[a], gb_ref)
 
-    def zone(a, hooks):
+    def begin(a):
         for copy in arrivals[a]:
             copy.wait()
         first = nn(place0_ref[...], land[a, 0:LAT1, :]).astype(BF)
         second = nn(place1_ref[...], land[a, LAT1:ROWS, :]).astype(BF)
         xw = jnp.concatenate([first[:, 0:C], second[:, 0:C]], axis=0)
         cw = jnp.concatenate([first[:, C:], second[:, C:]], axis=0)
-        gi = zone_step(a, xw, cw, g1, g2, wq, wk, wv, wit, wo_ref, wu_ref, wdt_ref,
-                       bias, masked, probs, dscores, mixed, dbias, hooks)
+        return zone_scores(a, xw, cw, g1, g2, wq, wk, wv, wit, wo_ref, wu_ref, wdt_ref, bias,
+                           masked.at[a], probs.at[a], dscores.at[a], mixed.at[a], dbias)
+
+    def finish(a, state):
+        gi = zone_finish(state, g1, wq, wk, wv, wo_ref, probs.at[a], dscores.at[a])
         first = nn(unplace0_ref[...], gi[0:N]).astype(BF)
         second = nn(unplace1_ref[...], gi[N:]).astype(BF)
         back_land[a, 0:LAT0, :] = first[0:LAT0]
@@ -461,13 +475,19 @@
         for p in range(2):
             gx_ref[(2 * a + 1 + p) % 4] = nn(unpack_ref[p], back_land[a]).astype(BF)
 
-    back0 = zone(0, {"scores": lambda: sum_first(0)})
-    back1 = zone(1, {"attended": lambda: sum_second(0), "tail": lambda: sum_third(0), "scores": lambda: sum_first(1)})
+    state0 = begin(0)
+    sum_first(0)
+    state1 = begin(1)
+    sum_first(1)
+    sum_second(0)
+    back0 = finish(0, state0)
+    back1 = finish(1, state1)
+    sum_second(1)
+    sum_third(0)
     collect(0, back0)
-    sum_last(0)
-    sum_second(1)
     collect(1, back1)
     sum_third(1)
+    sum_last(0)
     sum_last(1)
 
 

time: 56.5 us -> 49.1 us (0.87)
  Pallas kernels: 50.2 us -> 42.8 us
    pallas_call x1, Pallas kernels: 50.2 us -> 42.8 us  [block_call(): pl.pallas_call(block_kernel, out_shape=(jax.ShapeDtypeStruct((4, N, C), B...]
where the time goes in v3:
time: 49.1 us; the launch traced here: 48.8 us
  Pallas kernels  42.8 us (87%)
  local copies, waits for them, and re-layouts  5.36 us (11%)
  between operations  0.64 us (1%)
    pallas_call x1, Pallas kernels, block_call(): pl.pallas_call(block_kernel, out_shape=(jax.ShapeDtypeStruct((4, N, C), B...  42.8 us
    unnamed x3, local copies, waits for them, and re-layouts  5.36 us

profile of v3, /device:TPU:32, one launch (start us, length us, event | category | flops | bytes accessed | tf_op | source)
XLA Modules:
  0.0 48.8 jit_solution(1358363971950036135)
XLA Ops:
  0.6 1.7 %copy.20 = f32[2,1,6,23,144]{4,3,1,2,0:T(8,128)} copy(f32[2,1,6,23,144]{4,1,3,2,0:T(1,128)} %param.25) | data formatting | bytes 317952
  2.3 42.8 %shard_map.176 = (bf16[4,144,192]{2,1,0:T(8,128)(2,1)}, f32[12,23,144]{2,1,0:T(8,128)}) custom-call(bf16[4,144,192]{2,1,0:T(8,128)(2,1)} %bitcast.9, bf16[4,144,192]{2,1,0:T(8,128)(2,1)} %bitcast.10, bf16[2,352,144]{2,1,0:T(8,128)(2,1)} %constant.16.clone.refs_2_, bf16[144,160]{1,0:T(8,128)(2,1)} %constant.17.clone.refs_3_, ...), custom_call_target="tpu_custom_call" | custom-call | tf_op jit(solution)/shard_map/pallas_call | solution.py:497
  45.1 2.0 %copy.19 = f32[2,1,6,23,144]{4,1,3,2,0:T(1,128)} copy(f32[2,1,6,23,144]{4,3,2,0,1:T(8,128)} %bitcast.13) | data formatting | bytes 317952
  47.1 1.7 %copy.22 = bf16[4,6,24,192]{3,2,1,0:T(8,128)(2,1)} copy(bf16[4,6,24,192]{3,2,1,0:T(8,128)(2,1)} %bitcast.12) | data formatting | bytes 442368

commit v4 on v3

v4 whole, which is shorter than its diff:
```python
import functools
import numpy as np
import jax
import jax.numpy as jnp
from jax import lax
from jax.experimental import pallas as pl
from jax.experimental.pallas import tpu as pltpu

BF = jnp.bfloat16
F32 = jnp.float32
HEADS, WZ, WH, WW = 6, 2, 6, 12
HD = 32
C = 192
FF = 768
N = 144
PS = WZ * WH
OFFS = 2 * WW - 1
LW = 384
EPS = 1e-05
SCALE = HD ** -0.5
NEG = -1e30
LOG2E = 1.4426950408889634


def nn(a, b):
    return lax.dot_general(a, b, (((1,), (0,)), ((), ())), preferred_element_type=F32)


def nt(a, b):
    return lax.dot_general(a, b, (((1,), (1,)), ((), ())), preferred_element_type=F32)


def tn(a, b):
    return lax.dot_general(a, b, (((0,), (0,)), ((), ())), preferred_element_type=F32)


def fold_consts():
    join = np.zeros((LW, N), np.float32)
    own = np.zeros((16, N), np.float32)
    for p in range(WZ):
        for q in range(WZ):
            for s in range(WH):
                for t in range(WH):
                    m = ((p * WZ + q) * WH + s) * WH + t
                    own[q * WH + t, m] = 1
                    join[p * WH + s:OFFS * PS:PS, m] = 1
    pick = np.zeros((24, LW), np.float32)
    for r in range(OFFS):
        pick[r, r * PS:(r + 1) * PS] = 1
    return join, own, pick


def normalize(v):
    centred = v - jnp.mean(v, axis=-1, keepdims=True)
    rs = lax.rsqrt(jnp.mean(centred * centred, axis=-1, keepdims=True) + EPS)
    return centred * rs, rs


def norm_back(g, xh, rs):
    return rs * (g - jnp.mean(g, axis=-1, keepdims=True) - xh * jnp.mean(g * xh, axis=-1, keepdims=True))


def gelu_slope(h):
    cdf = 0.5 + 0.5 * lax.erf(h * 0.7071067811865476)
    return cdf + h * (jnp.exp(-0.5 * (h * h)) * 0.3989422804014327)


def expand_bias(lat, joint_ref, own_ref, pick_ref, t24, strips, bias):
    table = t24[...].reshape(12 * 24, N)
    hi = table.astype(BF)
    rest = table - hi.astype(F32)
    mid = rest.astype(BF)
    low = (rest - mid.astype(F32)).astype(BF)
    pick = pick_ref[...][None] * LOG2E
    for qt in range(PS):
        own = own_ref[qt:qt + 1, :]
        wide = nn(hi * own, joint_ref[...]) + nn(mid * own, joint_ref[...]) + nn(low * own, joint_ref[...])
        strips[:, qt, :] = jnp.sum(wide.reshape(12, 24, LW) * pick, axis=1)
    row = lax.broadcasted_iota(jnp.int32, (N, N), 0).astype(F32)
    col = lax.broadcasted_iota(jnp.int32, (N, N), 1).astype(F32)

    def place(v):
        ps = v - PS * jnp.floor((v + 0.5) * (1.0 / PS))
        upper = (ps >= WH).astype(F32)
        s = ps - WH * upper
        return upper, (s >= WH // 2).astype(F32)

    rp, rs = place(row)
    cp, cs = place(col)
    last_band = (lat == 3).astype(F32)
    apart_rows = jnp.abs(rs - cs) * last_band
    apart_levels = jnp.abs(rp - cp)
    for a in range(2):
        apart = apart_rows + apart_levels if a else apart_rows
        excluded = jnp.where(apart > 0.5, NEG, 0.0)
        for an in range(a * HEADS, (a + 1) * HEADS):
            strip = strips[an, 0:PS, :]
            for j in range(WW):
                lo = (WW - 1 - j) * PS
                rows = slice(j * PS, (j + 1) * PS)
                bias[an, rows, :] = strip[:, lo:lo + N] + excluded[rows]


GROUPS = ((0, 4), (4, 6))


def head_picks():
    lane = lax.broadcasted_iota(jnp.int32, (1, 128), 1)
    return [((lane >= n * HD % 128) & (lane < n * HD % 128 + HD)).astype(F32) for n in range(HEADS)]


WINDOWS = [slice(w * N, (w + 1) * N) for w in range(4)]


def all_scores(x, late_ct, g1, g2, wq, wk, wv, wqkvt, wo_ref, wu_ref, wdt_ref,
               bias, masked, probs, dscores, mixed, dbias, after_group):
    picks16 = [v.astype(BF) for v in head_picks()]

    def by_head(w, v, kind):
        for n in range(HEADS):
            if n < 4:
                masked[kind, w, n * N:(n + 1) * N, :] = v[:, 0:128] * picks16[n]
            else:
                masked[kind, w, n * N:(n + 1) * N, 0:64] = v[:, 128:C] * picks16[n][:, 0:64]

    x = x.astype(F32)
    xh1, rs1 = normalize(x)
    xn1 = (xh1 * g1).astype(BF)
    keys = nn(xn1, wk[...]).astype(BF)
    values = nn(xn1, wv[...]).astype(BF)
    qkvt = [nt(wqkvt[...], xn1[rows]).astype(BF) for rows in WINDOWS]
    for w, rows in enumerate(WINDOWS):
        by_head(w, keys[rows], 0)
        by_head(w, values[rows], 1)
    for first, end in GROUPS:
        width = min(C, end * HD) - first * HD
        for w in range(4):
            s_all = nn(masked[0, w, first * N:end * N, 0:width], qkvt[w][first * HD:end * HD, :])
            for n in range(first, end):
                s = s_all[(n - first) * N:(n - first + 1) * N] * (SCALE * LOG2E) + bias[(w // 2) * HEADS + n]
                e = jnp.exp2(s - jnp.max(s, axis=0, keepdims=True))
                p = (e * (1.0 / jnp.sum(e, axis=0, keepdims=True))).astype(BF)
                probs[w, n * N:(n + 1) * N, :] = p
                mixed[w, n * HD:(n + 1) * HD, :] = nn(qkvt[w][2 * C + n * HD:2 * C + (n + 1) * HD], p).astype(BF)
    ct = late_ct()
    attn = jnp.concatenate([tn(mixed[w], wo_ref[...]) for w in range(4)], axis=0).astype(BF)
    y = x + attn.astype(F32)
    xh2, rs2 = normalize(y)
    xn2 = (xh2 * g2).astype(BF)
    dxn2 = jnp.zeros((4 * N, C), F32)
    for f in range(FF // 256):
        up = wu_ref[:, f * 256:(f + 1) * 256]
        h = nn(xn2, up)
        da = nn(ct, wdt_ref[:, f * 256:(f + 1) * 256])
        dh = (da * gelu_slope(h)).astype(BF)
        dxn2 = dxn2 + nt(dh, up)
    dy = ct.astype(F32) + norm_back(dxn2 * g2, xh2, rs2)
    gattn = dy.astype(BF)
    dmixt = [nt(wo_ref[...], gattn[rows]).astype(BF) for rows in WINDOWS]
    for group, (first, end) in enumerate(GROUPS):
        width = min(C, end * HD) - first * HD
        span = slice(first * HD, first * HD + width)
        parts = [[], [], [], []]
        for w in range(4):
            dp_all = nn(masked[1, w, first * N:end * N, 0:width], dmixt[w][span, :])
            for n in range(first, end):
                dp = dp_all[(n - first) * N:(n - first + 1) * N]
                p = probs[w, n * N:(n + 1) * N, :].astype(F32)
                pd = p * dp
                ds = pd - p * jnp.sum(pd, axis=0, keepdims=True)
                parts[w].append(ds)
                dscores[w, n * N:(n + 1) * N, :] = ds.astype(BF)
            if w % 2:
                for n in range(first, end):
                    dbias[(w // 2) * HEADS + n] = parts[w - 1][n - first] + parts[w][n - first]
        after_group(group)
    return xh1, rs1, xn1, [v[C:2 * C] for v in qkvt], dy, gattn


def all_finish(state, g1, wq, wk, wv, wo_ref, probs, dscores, halfway):
    picks = head_picks()
    xh1, rs1, xn1, keyst, dy, gattn = state
    queries = nn(xn1, wq[...]).astype(BF)
    dmix = nt(gattn, wo_ref[...]).astype(BF)
    dqs, dks, dvs = [[], [], [], []], [[], [], [], []], [[], [], [], []]
    for first, end in GROUPS:
        width = min(C, end * HD) - first * HD
        span = slice(first * HD, first * HD + width)
        for w, rows in enumerate(WINDOWS):
            for n in range(first, end):
                dqs[w].append(nn(keyst[w][n * HD:(n + 1) * HD], dscores[w, n * N:(n + 1) * N, :]))
            dk_all = nn(dscores[w, first * N:end * N, :], queries[rows, span])
            dv_all = nn(probs[w, first * N:end * N, :], dmix[rows, span])
            for store, full in ((dks, dk_all), (dvs, dv_all)):
                total = jnp.zeros((N, width), F32)
                for n in range(first, end):
                    total = total + full[(n - first) * N:(n - first + 1) * N] * picks[n][:, 0:width]
                store[w].append(total)
    halfway()
    dq = jnp.concatenate([(jnp.concatenate(dqs[w], axis=0) * SCALE).astype(BF).T for w in range(4)], axis=0)
    dk = (jnp.concatenate([jnp.concatenate(dks[w], axis=1) for w in range(4)], axis=0) * SCALE).astype(BF)
    dv = jnp.concatenate([jnp.concatenate(dvs[w], axis=1) for w in range(4)], axis=0).astype(BF)
    dxn1 = nt(dq, wq[...]) + nt(dk, wk[...]) + nt(dv, wv[...])
    return (dy + norm_back(dxn1.astype(BF).astype(F32) * g1, xh1, rs1)).astype(BF)


def group_tables(group):
    first, end = GROUPS[group]
    return [a * HEADS + n for a in range(2) for n in range(first, end)]


def fold_bias(group, dbias, join_ref, own_ref, pick_ref, strips, red):
    tables = group_tables(group)
    count = len(tables)
    for k, an in enumerate(tables):
        total = jnp.zeros((PS, LW), F32)
        for j in range(WW):
            lo = (WW - 1 - j) * PS
            total = total + jnp.pad(dbias[an, j * PS:(j + 1) * PS, :], ((0, 0), (lo, LW - N - lo)))
        strips[k, 0:PS, :] = total
    total = jnp.zeros((count * 24, N), F32)
    for qt in range(PS):
        rows = (strips[0:count, qt, :][:, None, :] * pick_ref[...][None]).reshape(count * 24, LW).astype(BF)
        total = total + nn(rows, join_ref[...]) * own_ref[qt:qt + 1, :].astype(F32)
    tails = jnp.zeros((24, 128), F32)
    for k in range(count):
        tail = jnp.concatenate([total[k * 24:(k + 1) * 24, 128:N], jnp.zeros((24, 112), F32)], axis=1)
        tails = tails + (pltpu.roll(tail, 16 * k, 1) if k else tail)
    rows = red.shape[0] * red.shape[1]
    red[...] = jnp.concatenate(
        [total[:, 0:128], tails, jnp.zeros((rows - (count + 1) * 24, 128), F32)], axis=0).astype(BF).reshape(red.shape)


def unpack_fold(group, full, gb_ref):
    tables = group_tables(group)
    count = len(tables)
    rows = full[...].astype(F32).reshape(full.shape[0] * full.shape[1], 128)
    for k, an in enumerate(tables):
        place = slice(an * OFFS, (an + 1) * OFFS)
        gb_ref[place, 0, 0:128] = rows[k * 24:k * 24 + OFFS]
        gb_ref[place, 0, 128:N] = rows[count * 24:count * 24 + OFFS, 16 * k:16 * (k + 1)]


def prepare_weights(wi_ref, wit, wq, wk, wv):
    wit[...] = wi_ref[...].T
    for k, ref in enumerate((wq, wk, wv)):
        ref[...] = wi_ref[:, k * C:(k + 1) * C]


VM = pl.BlockSpec(memory_space=pltpu.VMEM)

MAIN_SCRATCH = [
    pltpu.VMEM((12, 24, N), F32),
    pltpu.VMEM((12, 16, LW), F32),
    pltpu.VMEM((12, N, N), F32),
    pltpu.VMEM((3 * C, C), BF),
    pltpu.VMEM((C, C), BF),
    pltpu.VMEM((C, C), BF),
    pltpu.VMEM((C, C), BF),
    pltpu.VMEM((2, 4, HEADS * N, 128), BF),
    pltpu.VMEM((4, HEADS * N, N), BF),
    pltpu.VMEM((4, HEADS * N, N), BF),
    pltpu.VMEM((4, C, N), BF),
    pltpu.VMEM((12, N, N), F32),
]


PIECE0, PIECE1 = 80, 48
LAT0, LAT1, OWN1, LON1, DIAG1, ROWS = 80, 160, 208, 256, 304, 352
MESH = pl.DeviceIdType.MESH


def piece_consts():
    pack = np.zeros((2, ROWS, N), np.float32)
    place0 = np.zeros((N, LAT1), np.float32)
    place1 = np.zeros((N, ROWS - LAT1), np.float32)
    for p in range(2):
        for h in range(6):
            own = h >= 3
            s = h - 3 if own else h + 3
            for w in range(24):
                e = (w - 6) % 24
                if e < 12:
                    row = (0 if own else LAT0) + (e * 2 + p) * 3 + s % 3
                    place0[e * PS + p * WH + s, row] = 1
                else:
                    e -= 12
                    base = (OWN1 if own else LAT1) if e < 6 else (LON1 if own else DIAG1)
                    row = base + ((e % 6) * 2 + p) * 3 + s % 3
                    place1[e * PS + p * WH + s, row - LAT1] = 1
                pack[p, row, h * 24 + w] = 1
    return pack, place0, place1


def lat_lon():
    return lax.axis_index("lat"), lax.axis_index("lon")


def shifted(lat, lon, da, do):
    return lax.rem(lat + 4 + da, 4), lax.rem(lon + 64 + do, 64)


def halo_copies(plan, box, land, lat, lon, send_sem, recv_sem):
    return [
        pltpu.make_async_remote_copy(
            src_ref=box.at[pl.ds(start, size)],
            dst_ref=land.at[pl.ds(target, size)],
            send_sem=send_sem.at[k],
            recv_sem=recv_sem.at[k],
            device_id=shifted(lat, lon, *step),
            device_id_type=MESH,
        )
        for k, (start, size, target, step) in enumerate(plan)
    ]


IN_PLAN = ((0, 128, LAT0, (-1, 0)), (128, 48, LON1, (0, -1)), (176, 48, DIAG1, (-1, -1)))
BACK_PLAN = ((LAT0, 128, LAT0, (1, 0)), (LON1, 48, LON1, (0, 1)), (DIAG1, 48, DIAG1, (1, 1)))


def deep_peer(lon, d):
    high, z, y = lon // 32, lax.rem(lon // 4, 8), lax.rem(lon, 4)
    return (high * 8 + lax.rem(z + d, 8)) * 4 + y


def plane_place(lon):
    return (lon // 32) * 4 + lax.rem(lon, 4)


def flat_peer(lon, d):
    z = lax.rem(lon // 4, 8)
    place = lax.rem(plane_place(lon) + d, 8)
    return ((place // 4) * 8 + z) * 4 + lax.rem(place, 4)


def sum_copies(kind, lon, lat, src, dst, send_sem, recv_sem):
    place = plane_place(lon)
    copies = []
    for d in (4, 3, 5, 2, 6, 1, 7) if kind == 1 else (6, 2, 5, 7, 4, 1, 3):
        if kind == 0:
            peer, source, target = flat_peer(lon, d), src.at[lax.rem(place + d, 8)], dst.at[d - 1]
        elif kind == 1:
            peer, source, target = deep_peer(lon, d), src, dst.at[d - 1]
        else:
            peer, source, target = flat_peer(lon, d), src, dst.at[place]
        copies.append(pltpu.make_async_remote_copy(
            src_ref=source, dst_ref=target, send_sem=send_sem.at[kind, d - 1], recv_sem=recv_sem.at[kind, d - 1],
            device_id=(lat, peer), device_id_type=MESH))
    return copies


def add_up(own, slots):
    total = own.astype(F32)
    for d in range(7):
        total = total + slots[d].astype(F32)
    return total.astype(BF)


LOCAL = (
    ((4, N, C), BF), ((4, N, C), BF), ((2, ROWS, N), BF), ((N, LAT1), BF), ((N, ROWS - LAT1), BF),
    ((12 * OFFS, 1, N), F32), ((1, C), F32), ((1, C), F32), ((C, 3 * C), BF), ((C, C), BF), ((C, FF), BF), ((C, FF), BF),
    ((LW, N), BF), ((N, LW), BF), ((16, N), BF), ((24, LW), F32), ((2, N, ROWS), BF), ((LAT1, N), BF), ((ROWS - LAT1, N), BF),
)


def block_kernel(*refs):
    count = len(LOCAL)
    far = refs[:count]
    gx_ref, gb_ref = refs[count:count + 2]
    near = refs[count + 2:2 * count + 2]
    (x_ref, ct_ref, pack_ref, place0_ref, place1_ref, tb_ref, g1_ref, g2_ref, wi_ref, wo_ref, wu_ref, wdt_ref,
     join_ref, joint_ref, own_ref, pick_ref, unpack_ref, unplace0_ref, unplace1_ref) = near
    (t24, strips, bias, wit, wq, wk, wv, masked, probs, dscores, mixed, dbias,
     out_box, land, back_box, back_land, *rest) = refs[2 * count + 2:]
    buffers, rest = (rest[0:6], rest[6:12]), rest[12:]
    near_sem, in_send, in_recv, back_send, back_recv, sum_send, sum_recv = rest
    lat, lon = lat_lon()
    mine = plane_place(lon)

    barrier = pltpu.get_barrier_semaphore()
    for da, do in ((1, 0), (0, 1), (1, 1), (-1, 0), (0, -1), (-1, -1)):
        pl.semaphore_signal(barrier, inc=1, device_id=shifted(lat, lon, da, do), device_id_type=MESH)
    fetches = [pltpu.make_async_copy(far[k], near[k], near_sem.at[k]) for k in range(count)]
    for fetch in fetches:
        fetch.start()
    for d in range(1, 8):
        pl.semaphore_signal(barrier, inc=1, device_id=(lat, deep_peer(lon, d)), device_id_type=MESH)
        pl.semaphore_signal(barrier, inc=1, device_id=(lat, flat_peer(lon, d)), device_id_type=MESH)
    for fetch in fetches[0:3]:
        fetch.wait()

    arrivals = []
    for k, ref in enumerate((x_ref, ct_ref)):
        for a in range(2):
            piece = (nn(pack_ref[0], ref[(2 * a + 1) % 4]) + nn(pack_ref[1], ref[(2 * a + 2) % 4])).astype(BF)
            lanes = slice(a * C, (a + 1) * C)
            land[k, 0:LAT0, lanes] = piece[0:LAT0]
            land[k, OWN1:LON1, lanes] = piece[OWN1:LON1]
            out_box[k, 0:128, lanes] = piece[LAT0:OWN1]
            out_box[k, 128:224, lanes] = piece[LON1:ROWS]
        if k == 0:
            pl.semaphore_wait(barrier, 20)
        arrivals.append(halo_copies(IN_PLAN, out_box.at[k], land.at[k], lat, lon, in_send.at[k], in_recv.at[k]))
        for copy in arrivals[k]:
            copy.start()

    for fetch in fetches[3:]:
        fetch.wait()
    t24[...] = jnp.zeros_like(t24)
    for an in range(12):
        t24[an, 0:OFFS, :] = tb_ref[an * OFFS:(an + 1) * OFFS, 0, :]
    prepare_weights(wi_ref, wit, wq, wk, wv)
    expand_bias(lat, joint_ref, own_ref, pick_ref, t24, strips, bias)
    g1, g2 = g1_ref[...], g2_ref[...]

    sums = []
    for g, (red, slots1, part, slots2, whole, full) in enumerate(buffers):
        sums.append([sum_copies(kind, lon, lat, src, dst, sum_send.at[g], sum_recv.at[g])
                     for kind, (src, dst) in enumerate(((red, slots1), (part, slots2), (whole, full)))])

    def sum_first(g):
        fold_bias(g, dbias, join_ref, own_ref, pick_ref, strips, buffers[g][0])
        for copy in sums[g][0]:
            copy.start()

    def sum_second(g):
        red, slots1, part = buffers[g][0:3]
        for copy in sums[g][0]:
            copy.wait_recv()
        part[...] = add_up(red[mine], slots1)
        for copy in sums[g][1]:
            copy.start()

    def sum_third(g):
        part, slots2, whole, full = buffers[g][2:6]
        for copy in sums[g][1]:
            copy.wait_recv()
        whole[...] = add_up(part[...], slots2)
        for copy in sums[g][2]:
            copy.start()
        full[mine] = whole[...]

    def sum_last(g):
        for copy in sums[g][2]:
            copy.wait_recv()
        unpack_fold(g, buffers[g][5], gb_ref)

    def windows(k):
        for copy in arrivals[k]:
            copy.wait()
        first = nn(place0_ref[...], land[k, 0:LAT1, :]).astype(BF)
        second = nn(place1_ref[...], land[k, LAT1:ROWS, :]).astype(BF)
        return jnp.concatenate([v[:, a * C:(a + 1) * C] for a in range(2) for v in (first, second)], axis=0)

    state = all_scores(windows(0), lambda: windows(1), g1, g2, wq, wk, wv, wit, wo_ref, wu_ref, wdt_ref, bias,
                       masked, probs, dscores, mixed, dbias, sum_first)
    gi = all_finish(state, g1, wq, wk, wv, wo_ref, probs, dscores, lambda: sum_second(0))
    for a in range(2):
        lanes = slice(a * C, (a + 1) * C)
        first = nn(unplace0_ref[...], gi[WINDOWS[2 * a]]).astype(BF)
        second = nn(unplace1_ref[...], gi[WINDOWS[2 * a + 1]]).astype(BF)
        back_land[0:LAT0, lanes] = first[0:LAT0]
        back_land[OWN1:LON1, lanes] = second[OWN1 - LAT1:LON1 - LAT1]
        back_box[LAT0:LAT1, lanes] = first[LAT0:LAT1]
        back_box[LAT1:OWN1, lanes] = second[0:OWN1 - LAT1]
        back_box[LON1:ROWS, lanes] = second[LON1 - LAT1:]
    returns = halo_copies(BACK_PLAN, back_box, back_land, lat, lon, back_send, back_recv)
    for copy in returns:
        copy.start()
    sum_second(1)
    sum_third(0)
    sum_third(1)
    for copy in returns:
        copy.wait()
    for a in range(2):
        for p in range(2):
            gx_ref[(2 * a + 1 + p) % 4] = nn(unpack_ref[p], back_land[:, a * C:(a + 1) * C]).astype(BF)
    sum_last(0)
    for chain in sums:
        for phase in chain[0:2]:
            for copy in phase:
                copy.wait_send()
    sum_last(1)
    for chain in sums:
        for copy in chain[2]:
            copy.wait_send()


def sum_buffers(rows):
    return [pltpu.VMEM(lead + (rows, 128), BF) for lead in ((8,), (7,), (), (7,), (), (8,))]


def block_call(*operands):
    anywhere = pl.BlockSpec(memory_space=pl.ANY)
    dma = pltpu.SemaphoreType.DMA
    return pl.pallas_call(
        block_kernel,
        out_shape=(pltpu.VMEM((4, N, C), BF), pltpu.VMEM((12 * OFFS, 1, N), F32)),
        in_specs=[anywhere] * len(LOCAL),
        out_specs=(VM, VM),
        scratch_shapes=[pltpu.VMEM(*one) for one in LOCAL] + MAIN_SCRATCH + [
            pltpu.VMEM((2, 224, 2 * C), BF),
            pltpu.VMEM((2, ROWS, 2 * C), BF),
            pltpu.VMEM((ROWS, 2 * C), BF),
            pltpu.VMEM((ROWS, 2 * C), BF),
        ] + sum_buffers(32) + sum_buffers(16) + [
            dma((len(LOCAL),)), dma((2, 3)), dma((2, 3)), dma((3,)), dma((3,)), dma((2, 3, 7)), dma((2, 3, 7)),
        ],
        compiler_params=pltpu.CompilerParams(collective_id=0, has_side_effects=True, vmem_limit_bytes=60 * 1024 * 1024),
    )(*operands)


def on_device(block_input, cotangent, first_gain, second_gain, input_weight, output_weight, up_weight,
              down_weight, bias_table):
    join, own, pick = fold_consts()
    pack, place0, place1 = piece_consts()
    as_bf = lambda v: jnp.asarray(v, BF)
    gx, gb = block_call(
        block_input.reshape(4, N, C), cotangent.reshape(4, N, C), as_bf(pack), as_bf(place0), as_bf(place1),
        bias_table.reshape(12 * OFFS, 1, N),
        first_gain[None], second_gain[None], input_weight, output_weight, up_weight, down_weight.T,
        as_bf(join), as_bf(join.T), as_bf(own), jnp.asarray(pick), as_bf(pack.transpose(0, 2, 1)), as_bf(place0.T), as_bf(place1.T))
    return gx.reshape(block_input.shape), gb.reshape(bias_table.shape)


def solution(mesh):
    P = jax.sharding.PartitionSpec
    in_specs = (
        P(None, "lat", "lon", None),
        P(None, "lat", "lon", None),
        P(), P(), P(), P(), P(), P(),
        P(None, "lat", None, None, None),
    )
    out_specs = (P(None, "lat", "lon", None), P(None, "lat", None, None, None))
    return jax.shard_map(on_device, mesh=mesh, in_specs=in_specs, out_specs=out_specs, check_vma=False)
```

time: 49.1 us -> 41.6 us (0.85)
  local copies, waits for them, and re-layouts: 5.36 us -> 1.43 us
  Pallas kernels: 42.8 us -> 39.1 us
    unnamed x3 -> x2, local copies, waits for them, and re-layouts: 5.36 us -> 1.43 us
    pallas_call x1, Pallas kernels: 42.8 us -> 39.1 us  [block_call(): pl.pallas_call(block_kernel, out_shape=(pltpu.VMEM((4, N, C), BF), pltpu....]
where the time goes in v4:
time: 41.6 us; the launch traced here: 41.2 us
  Pallas kernels  39.1 us (94%)
  local copies, waits for them, and re-layouts  1.43 us (3%)
  between operations  0.64 us (2%)
    pallas_call x1, Pallas kernels, block_call(): pl.pallas_call(block_kernel, out_shape=(pltpu.VMEM((4, N, C), BF), pltpu....  39.1 us
    unnamed x2, local copies, waits for them, and re-layouts  1.43 us

profile of v4, /device:TPU:32, one launch (start us, length us, event | category | flops | bytes accessed | tf_op | source)
XLA Modules:
  0.0 41.2 jit_solution(11128634272303243587)
XLA Ops:
  0.6 39.1 %shard_map.194 = (bf16[4,144,192]{2,1,0:T(8,128)(2,1)S(1)}, f32[276,1,144]{2,1,0:T(1,128)S(1)}) custom-call(bf16[4,144,192]{2,1,0:T(8,128)(2,1)} %bitcast.10, bf16[4,144,192]{2,1,0:T(8,128)(2,1)} %bitcast.11, bf16[2,352,144]{2,1,0:T(8,128)(2,1)} %constant.20.clone.refs_2_, bf16[144,160]{1,0:T(8,128)(2,1)} %constant.21.clone.refs_3_, ...), custom_call_target="tpu_custom_call" | custom-call | tf_op jit(solution)/shard_map/pallas_call | solution.py:496
  39.7 0.7 %copy.23 = bf16[4,6,24,192]{3,2,1,0:T(8,128)(2,1)} copy(bf16[4,6,24,192]{3,2,1,0:T(8,128)(2,1)S(1)} %bitcast.8) | data formatting | bytes 442368
  40.5 0.7 %copy.24 = f32[2,1,6,23,144]{4,1,3,2,0:T(1,128)} copy(f32[2,1,6,23,144]{4,1,3,2,0:T(1,128)S(1)} %bitcast.9) | data formatting | bytes 317952

commit v5 on v4

--- a/solution.py
+++ b/solution.py
@@ -68,13 +68,11 @@
 def expand_bias(lat, joint_ref, own_ref, pick_ref, t24, strips, bias):
     table = t24[...].reshape(12 * 24, N)
     hi = table.astype(BF)
-    rest = table - hi.astype(F32)
-    mid = rest.astype(BF)
-    low = (rest - mid.astype(F32)).astype(BF)
+    low = (table - hi.astype(F32)).astype(BF)
     pick = pick_ref[...][None] * LOG2E
     for qt in range(PS):
         own = own_ref[qt:qt + 1, :]
-        wide = nn(hi * own, joint_ref[...]) + nn(mid * own, joint_ref[...]) + nn(low * own, joint_ref[...])
+        wide = nn(hi * own, joint_ref[...]) + nn(low * own, joint_ref[...])
         strips[:, qt, :] = jnp.sum(wide.reshape(12, 24, LW) * pick, axis=1)
     row = lax.broadcasted_iota(jnp.int32, (N, N), 0).astype(F32)
     col = lax.broadcasted_iota(jnp.int32, (N, N), 1).astype(F32)
@@ -113,7 +111,7 @@
 
 
 def all_scores(x, late_ct, g1, g2, wq, wk, wv, wqkvt, wo_ref, wu_ref, wdt_ref,
-               bias, masked, probs, dscores, mixed, dbias, after_group):
+               bias, masked, blocks, probs, dscores, mixed, dbias, after_group):
     picks16 = [v.astype(BF) for v in head_picks()]
 
     def by_head(w, v, kind):
@@ -132,6 +130,10 @@
     for w, rows in enumerate(WINDOWS):
         by_head(w, keys[rows], 0)
         by_head(w, values[rows], 1)
+        for n in range(HEADS):
+            for k in range(2):
+                blocks[k, w, n * HD:(n + 1) * HD, n * N:(n + 1) * N] = (
+                    qkvt[w][(2 - k) * C + n * HD:(2 - k) * C + (n + 1) * HD])
     for first, end in GROUPS:
         width = min(C, end * HD) - first * HD
         for w in range(4):
@@ -141,7 +143,8 @@
                 e = jnp.exp2(s - jnp.max(s, axis=0, keepdims=True))
                 p = (e * (1.0 / jnp.sum(e, axis=0, keepdims=True))).astype(BF)
                 probs[w, n * N:(n + 1) * N, :] = p
-                mixed[w, n * HD:(n + 1) * HD, :] = nn(qkvt[w][2 * C + n * HD:2 * C + (n + 1) * HD], p).astype(BF)
+    for w in range(4):
+        mixed[w] = nn(blocks[0, w], probs[w]).astype(BF)
     ct = late_ct()
     attn = jnp.concatenate([tn(mixed[w], wo_ref[...]) for w in range(4)], axis=0).astype(BF)
     y = x + attn.astype(F32)
@@ -174,21 +177,20 @@
                 for n in range(first, end):
                     dbias[(w // 2) * HEADS + n] = parts[w - 1][n - first] + parts[w][n - first]
         after_group(group)
-    return xh1, rs1, xn1, [v[C:2 * C] for v in qkvt], dy, gattn
-
-
-def all_finish(state, g1, wq, wk, wv, wo_ref, probs, dscores, halfway):
+    return xh1, rs1, xn1, dy, gattn
+
+
+def all_finish(state, g1, wq, wk, wv, wo_ref, blocks, probs, dscores, halfway):
     picks = head_picks()
-    xh1, rs1, xn1, keyst, dy, gattn = state
+    xh1, rs1, xn1, dy, gattn = state
     queries = nn(xn1, wq[...]).astype(BF)
     dmix = nt(gattn, wo_ref[...]).astype(BF)
-    dqs, dks, dvs = [[], [], [], []], [[], [], [], []], [[], [], [], []]
+    dqs = [nn(blocks[1, w], dscores[w]) for w in range(4)]
+    dks, dvs = [[], [], [], []], [[], [], [], []]
     for first, end in GROUPS:
         width = min(C, end * HD) - first * HD
         span = slice(first * HD, first * HD + width)
         for w, rows in enumerate(WINDOWS):
-            for n in range(first, end):
-                dqs[w].append(nn(keyst[w][n * HD:(n + 1) * HD], dscores[w, n * N:(n + 1) * N, :]))
             dk_all = nn(dscores[w, first * N:end * N, :], queries[rows, span])
             dv_all = nn(probs[w, first * N:end * N, :], dmix[rows, span])
             for store, full in ((dks, dk_all), (dvs, dv_all)):
@@ -197,7 +199,7 @@
                     total = total + full[(n - first) * N:(n - first + 1) * N] * picks[n][:, 0:width]
                 store[w].append(total)
     halfway()
-    dq = jnp.concatenate([(jnp.concatenate(dqs[w], axis=0) * SCALE).astype(BF).T for w in range(4)], axis=0)
+    dq = jnp.concatenate([(dqs[w] * SCALE).astype(BF).T for w in range(4)], axis=0)
     dk = (jnp.concatenate([jnp.concatenate(dks[w], axis=1) for w in range(4)], axis=0) * SCALE).astype(BF)
     dv = jnp.concatenate([jnp.concatenate(dvs[w], axis=1) for w in range(4)], axis=0).astype(BF)
     dxn1 = nt(dq, wq[...]) + nt(dk, wk[...]) + nt(dv, wv[...])
@@ -258,6 +260,7 @@
     pltpu.VMEM((C, C), BF),
     pltpu.VMEM((C, C), BF),
     pltpu.VMEM((2, 4, HEADS * N, 128), BF),
+    pltpu.VMEM((2, 4, C, HEADS * N), BF),
     pltpu.VMEM((4, HEADS * N, N), BF),
     pltpu.VMEM((4, HEADS * N, N), BF),
     pltpu.VMEM((4, C, N), BF),
@@ -370,7 +373,7 @@
     near = refs[count + 2:2 * count + 2]
     (x_ref, ct_ref, pack_ref, place0_ref, place1_ref, tb_ref, g1_ref, g2_ref, wi_ref, wo_ref, wu_ref, wdt_ref,
      join_ref, joint_ref, own_ref, pick_ref, unpack_ref, unplace0_ref, unplace1_ref) = near
-    (t24, strips, bias, wit, wq, wk, wv, masked, probs, dscores, mixed, dbias,
+    (t24, strips, bias, wit, wq, wk, wv, masked, blocks, probs, dscores, mixed, dbias,
      out_box, land, back_box, back_land, *rest) = refs[2 * count + 2:]
     buffers, rest = (rest[0:6], rest[6:12]), rest[12:]
     near_sem, in_send, in_recv, back_send, back_recv, sum_send, sum_recv = rest
@@ -407,6 +410,7 @@
     for fetch in fetches[3:]:
         fetch.wait()
     t24[...] = jnp.zeros_like(t24)
+    blocks[...] = jnp.zeros_like(blocks)
     for an in range(12):
         t24[an, 0:OFFS, :] = tb_ref[an * OFFS:(an + 1) * OFFS, 0, :]
     prepare_weights(wi_ref, wit, wq, wk, wv)
@@ -453,8 +457,8 @@
         return jnp.concatenate([v[:, a * C:(a + 1) * C] for a in range(2) for v in (first, second)], axis=0)
 
     state = all_scores(windows(0), lambda: windows(1), g1, g2, wq, wk, wv, wit, wo_ref, wu_ref, wdt_ref, bias,
-                       masked, probs, dscores, mixed, dbias, sum_first)
-    gi = all_finish(state, g1, wq, wk, wv, wo_ref, probs, dscores, lambda: sum_second(0))
+                       masked, blocks, probs, dscores, mixed, dbias, sum_first)
+    gi = all_finish(state, g1, wq, wk, wv, wo_ref, blocks, probs, dscores, lambda: sum_second(0))
     for a in range(2):
         lanes = slice(a * C, (a + 1) * C)
         first = nn(unplace0_ref[...], gi[WINDOWS[2 * a]]).astype(BF)

time: 41.6 us -> 40.9 us (0.983)
  Pallas kernels: 39.1 us -> 38.3 us
    pallas_call x1, Pallas kernels: 39.1 us -> 38.3 us  [block_call(): pl.pallas_call(block_kernel, out_shape=(pltpu.VMEM((4, N, C), BF), pltpu....]
where the time goes in v5:
time: 40.9 us; the launch traced here: 40.4 us
  Pallas kernels  38.3 us (94%)
  local copies, waits for them, and re-layouts  1.43 us (3%)
  between operations  0.64 us (2%)
    pallas_call x1, Pallas kernels, block_call(): pl.pallas_call(block_kernel, out_shape=(pltpu.VMEM((4, N, C), BF), pltpu....  38.3 us
    unnamed x2, local copies, waits for them, and re-layouts  1.43 us

profile of v5, /device:TPU:32, one launch (start us, length us, event | category | flops | bytes accessed | tf_op | source)
XLA Modules:
  0.0 40.4 jit_solution(10350677165869555119)
XLA Ops:
  0.6 38.3 %shard_map.194 = (bf16[4,144,192]{2,1,0:T(8,128)(2,1)S(1)}, f32[276,1,144]{2,1,0:T(1,128)S(1)}) custom-call(bf16[4,144,192]{2,1,0:T(8,128)(2,1)} %bitcast.10, bf16[4,144,192]{2,1,0:T(8,128)(2,1)} %bitcast.11, bf16[2,352,144]{2,1,0:T(8,128)(2,1)} %constant.20.clone.refs_2_, bf16[144,160]{1,0:T(8,128)(2,1)} %constant.21.clone.refs_3_, ...), custom_call_target="tpu_custom_call" | custom-call | tf_op jit(solution)/shard_map/pallas_call | solution.py:500
  39.0 0.7 %copy.23 = bf16[4,6,24,192]{3,2,1,0:T(8,128)(2,1)} copy(bf16[4,6,24,192]{3,2,1,0:T(8,128)(2,1)S(1)} %bitcast.8) | data formatting | bytes 442368
  39.7 0.7 %copy.24 = f32[2,1,6,23,144]{4,1,3,2,0:T(1,128)} copy(f32[2,1,6,23,144]{4,1,3,2,0:T(1,128)S(1)} %bitcast.9) | data formatting | bytes 317952

commit v6 on v5

--- a/solution.py
+++ b/solution.py
@@ -211,19 +211,32 @@
     return [a * HEADS + n for a in range(2) for n in range(first, end)]
 
 
+def diagonals(an, dbias):
+    total = jnp.zeros((PS, LW), F32)
+    for j in range(WW):
+        lo = (WW - 1 - j) * PS
+        total = total + jnp.pad(dbias[an, j * PS:(j + 1) * PS, :], ((0, 0), (lo, LW - N - lo)))
+    return total
+
+
+def to_columns(count, rows_of, join_ref, own_ref, pick_ref):
+    total = jnp.zeros((count * 24, N), F32)
+    for qt in range(PS):
+        rows = (rows_of(qt)[:, None, :] * pick_ref[...][None]).reshape(count * 24, LW).astype(BF)
+        total = total + nn(rows, join_ref[...]) * own_ref[qt:qt + 1, :].astype(F32)
+    return total
+
+
 def fold_bias(group, dbias, join_ref, own_ref, pick_ref, strips, red):
     tables = group_tables(group)
     count = len(tables)
+    if group == 0:
+        for k, an in enumerate(tables):
+            red[k] = jnp.concatenate([diagonals(an, dbias), jnp.zeros((16 - PS, LW), F32)], axis=0).astype(BF)
+        return
     for k, an in enumerate(tables):
-        total = jnp.zeros((PS, LW), F32)
-        for j in range(WW):
-            lo = (WW - 1 - j) * PS
-            total = total + jnp.pad(dbias[an, j * PS:(j + 1) * PS, :], ((0, 0), (lo, LW - N - lo)))
-        strips[k, 0:PS, :] = total
-    total = jnp.zeros((count * 24, N), F32)
-    for qt in range(PS):
-        rows = (strips[0:count, qt, :][:, None, :] * pick_ref[...][None]).reshape(count * 24, LW).astype(BF)
-        total = total + nn(rows, join_ref[...]) * own_ref[qt:qt + 1, :].astype(F32)
+        strips[k, 0:PS, :] = diagonals(an, dbias)
+    total = to_columns(count, lambda qt: strips[0:count, qt, :], join_ref, own_ref, pick_ref)
     tails = jnp.zeros((24, 128), F32)
     for k in range(count):
         tail = jnp.concatenate([total[k * 24:(k + 1) * 24, 128:N], jnp.zeros((24, 112), F32)], axis=1)
@@ -233,9 +246,27 @@
         [total[:, 0:128], tails, jnp.zeros((rows - (count + 1) * 24, 128), F32)], axis=0).astype(BF).reshape(red.shape)
 
 
+def fold_one(strip, join_ref, own_ref, pick_ref):
+    total = to_columns(1, lambda qt: strip[qt:qt + 1], join_ref, own_ref, pick_ref)
+    tails = jnp.zeros((8, 128), F32)
+    for g in range(3):
+        tail = jnp.concatenate([total[8 * g:8 * g + 8, 128:N], jnp.zeros((8, 112), F32)], axis=1)
+        tails = tails + (pltpu.roll(tail, 16 * g, 1) if g else tail)
+    return jnp.concatenate([total[:, 0:128], tails], axis=0).astype(BF)
+
+
 def unpack_fold(group, full, gb_ref):
     tables = group_tables(group)
     count = len(tables)
+    if group == 0:
+        for k, an in enumerate(tables):
+            rows = full[k].astype(F32)
+            gb_ref[an * OFFS:(an + 1) * OFFS, 0, 0:128] = rows[0:OFFS]
+            for g in range(3):
+                size = min(8, OFFS - 8 * g)
+                place = slice(an * OFFS + 8 * g, an * OFFS + 8 * g + size)
+                gb_ref[place, 0, 128:N] = rows[24:24 + size, 16 * g:16 * (g + 1)]
+        return
     rows = full[...].astype(F32).reshape(full.shape[0] * full.shape[1], 128)
     for k, an in enumerate(tables):
         place = slice(an * OFFS, (an + 1) * OFFS)
@@ -356,7 +387,7 @@
     total = own.astype(F32)
     for d in range(7):
         total = total + slots[d].astype(F32)
-    return total.astype(BF)
+    return total
 
 
 LOCAL = (
@@ -431,7 +462,7 @@
         red, slots1, part = buffers[g][0:3]
         for copy in sums[g][0]:
             copy.wait_recv()
-        part[...] = add_up(red[mine], slots1)
+        part[...] = add_up(red[mine], slots1).astype(BF)
         for copy in sums[g][1]:
             copy.start()
 
@@ -439,7 +470,8 @@
         part, slots2, whole, full = buffers[g][2:6]
         for copy in sums[g][1]:
             copy.wait_recv()
-        whole[...] = add_up(part[...], slots2)
+        total = add_up(part[...], slots2)
+        whole[...] = total.astype(BF) if g else fold_one(total, join_ref, own_ref, pick_ref)
         for copy in sums[g][2]:
             copy.start()
         full[mine] = whole[...]
@@ -490,8 +522,9 @@
             copy.wait_send()
 
 
-def sum_buffers(rows):
-    return [pltpu.VMEM(lead + (rows, 128), BF) for lead in ((8,), (7,), (), (7,), (), (8,))]
+def sum_buffers(rows, lanes, whole_rows):
+    sent = [pltpu.VMEM(lead + (rows, lanes), BF) for lead in ((8,), (7,), (), (7,))]
+    return sent + [pltpu.VMEM(lead + (whole_rows, 128), BF) for lead in ((), (8,))]
 
 
 def block_call(*operands):
@@ -507,7 +540,7 @@
             pltpu.VMEM((2, ROWS, 2 * C), BF),
             pltpu.VMEM((ROWS, 2 * C), BF),
             pltpu.VMEM((ROWS, 2 * C), BF),
-        ] + sum_buffers(32) + sum_buffers(16) + [
+        ] + sum_buffers(16, LW, 32) + sum_buffers(16, 128, 16) + [
             dma((len(LOCAL),)), dma((2, 3)), dma((2, 3)), dma((3,)), dma((3,)), dma((2, 3, 7)), dma((2, 3, 7)),
         ],
         compiler_params=pltpu.CompilerParams(collective_id=0, has_side_effects=True, vmem_limit_bytes=60 * 1024 * 1024),

time: 40.9 us -> 40.4 us (0.988)
  Pallas kernels: 38.3 us -> 37.6 us
    pallas_call x1, Pallas kernels: 38.3 us -> 37.6 us  [block_call(): pl.pallas_call(block_kernel, out_shape=(pltpu.VMEM((4, N, C), BF), pltpu....]
where the time goes in v6:
time: 40.4 us; the launch traced here: 39.7 us
  Pallas kernels  37.6 us (93%)
  local copies, waits for them, and re-layouts  1.43 us (4%)
  between operations  0.64 us (2%)
    pallas_call x1, Pallas kernels, block_call(): pl.pallas_call(block_kernel, out_shape=(pltpu.VMEM((4, N, C), BF), pltpu....  37.6 us
    unnamed x2, local copies, waits for them, and re-layouts  1.43 us

profile of v6, /device:TPU:32, one launch (start us, length us, event | category | flops | bytes accessed | tf_op | source)
XLA Modules:
  0.0 39.7 jit_solution(10231360922912294810)
XLA Ops:
  0.6 37.6 %shard_map.194 = (bf16[4,144,192]{2,1,0:T(8,128)(2,1)S(1)}, f32[276,1,144]{2,1,0:T(1,128)S(1)}) custom-call(bf16[4,144,192]{2,1,0:T(8,128)(2,1)} %bitcast.10, bf16[4,144,192]{2,1,0:T(8,128)(2,1)} %bitcast.11, bf16[2,352,144]{2,1,0:T(8,128)(2,1)} %constant.20.clone.refs_2_, bf16[144,160]{1,0:T(8,128)(2,1)} %constant.21.clone.refs_3_, ...), custom_call_target="tpu_custom_call" | custom-call | tf_op jit(solution)/shard_map/pallas_call | solution.py:533
  38.3 0.7 %copy.23 = bf16[4,6,24,192]{3,2,1,0:T(8,128)(2,1)} copy(bf16[4,6,24,192]{3,2,1,0:T(8,128)(2,1)S(1)} %bitcast.8) | data formatting | bytes 442368
  39.0 0.7 %copy.24 = f32[2,1,6,23,144]{4,1,3,2,0:T(1,128)} copy(f32[2,1,6,23,144]{4,1,3,2,0:T(1,128)S(1)} %bitcast.9) | data formatting | bytes 317952

commit v7 on v6

--- a/solution.py
+++ b/solution.py
@@ -348,8 +348,8 @@
     ]
 
 
-IN_PLAN = ((0, 128, LAT0, (-1, 0)), (128, 48, LON1, (0, -1)), (176, 48, DIAG1, (-1, -1)))
-BACK_PLAN = ((LAT0, 128, LAT0, (1, 0)), (LON1, 48, LON1, (0, 1)), (DIAG1, 48, DIAG1, (1, 1)))
+IN_PLAN = ((176, 48, DIAG1, (-1, -1)), (128, 48, LON1, (0, -1)), (0, 128, LAT0, (-1, 0)))
+BACK_PLAN = ((DIAG1, 48, DIAG1, (1, 1)), (LON1, 48, LON1, (0, 1)), (LAT0, 128, LAT0, (1, 0)))
 
 
 def deep_peer(lon, d):
@@ -483,7 +483,7 @@
 
     def windows(k):
         for copy in arrivals[k]:
-            copy.wait()
+            copy.wait_recv()
         first = nn(place0_ref[...], land[k, 0:LAT1, :]).astype(BF)
         second = nn(place1_ref[...], land[k, LAT1:ROWS, :]).astype(BF)
         return jnp.concatenate([v[:, a * C:(a + 1) * C] for a in range(2) for v in (first, second)], axis=0)
@@ -507,11 +507,13 @@
     sum_third(0)
     sum_third(1)
     for copy in returns:
-        copy.wait()
+        copy.wait_recv()
     for a in range(2):
         for p in range(2):
             gx_ref[(2 * a + 1 + p) % 4] = nn(unpack_ref[p], back_land[:, a * C:(a + 1) * C]).astype(BF)
     sum_last(0)
+    for copy in arrivals[0] + arrivals[1] + returns:
+        copy.wait_send()
     for chain in sums:
         for phase in chain[0:2]:
             for copy in phase:

time: 40.4 us -> 40.1 us (level)
  no operation moved by 1% of the time
where the time goes in v7:
time: 40.1 us; the launch traced here: 39.7 us
  Pallas kernels  37.7 us (94%)
  local copies, waits for them, and re-layouts  1.43 us (4%)
  between operations  0.64 us (2%)
    pallas_call x1, Pallas kernels, block_call(): pl.pallas_call(block_kernel, out_shape=(pltpu.VMEM((4, N, C), BF), pltpu....  37.7 us
    unnamed x2, local copies, waits for them, and re-layouts  1.43 us

profile of v7, /device:TPU:32, one launch (start us, length us, event | category | flops | bytes accessed | tf_op | source)
XLA Modules:
  0.0 39.7 jit_solution(952501295674438336)
XLA Ops:
  0.6 37.7 %shard_map.194 = (bf16[4,144,192]{2,1,0:T(8,128)(2,1)S(1)}, f32[276,1,144]{2,1,0:T(1,128)S(1)}) custom-call(bf16[4,144,192]{2,1,0:T(8,128)(2,1)} %bitcast.10, bf16[4,144,192]{2,1,0:T(8,128)(2,1)} %bitcast.11, bf16[2,352,144]{2,1,0:T(8,128)(2,1)} %constant.20.clone.refs_2_, bf16[144,160]{1,0:T(8,128)(2,1)} %constant.21.clone.refs_3_, ...), custom_call_target="tpu_custom_call" | custom-call | tf_op jit(solution)/shard_map/pallas_call | solution.py:535
  38.3 0.7 %copy.23 = bf16[4,6,24,192]{3,2,1,0:T(8,128)(2,1)} copy(bf16[4,6,24,192]{3,2,1,0:T(8,128)(2,1)S(1)} %bitcast.8) | data formatting | bytes 442368
  39.0 0.7 %copy.24 = f32[2,1,6,23,144]{4,1,3,2,0:T(1,128)} copy(f32[2,1,6,23,144]{4,1,3,2,0:T(1,128)S(1)} %bitcast.9) | data formatting | bytes 317952
